TPU v7x, 256 devices: a whole 4x4x8 slice. The times are simulated.
256 devices in a mesh: tm: 32 (over z, x_hi, core), comp: 8 (over y, x_lo).
Axes of the slice: x: 4 (x_hi: 2, x_lo: 2; x = x_hi * 2 + x_lo), y: 4, z: 8, core: 2. Of those that a mesh axis runs over, the one named last changes fastest.
Arguments:
- velocities: bfloat16 [8192, 3, 4096], P('tm', None, 'comp'), may hold values from -6 to 6
- atom_mask: int32 [4096], P('comp'), may hold values 0 or 1
- valid_frames: int32 [1], replicated, may hold values from 7936 to 8192
Outputs:
- correlation: float32 [256, 4096], P('tm', 'comp')
- average: float32 [256], P('tm')
All inputs are finite; a program needn't handle non-finite values. No bound on the sum of `atom_mask` on one device may be relied on, other than what follows from the above.
Results may differ from a plain program's by a relative error of at most 0.0003.
Values may be sent and summed in bfloat16 or wider, within the bound.
No kernel may reach another device: no remote copies, remote signals or barrier semaphores. Data moves between devices by JAX's collectives and lax.ppermute only.
A program may use at most 64 MiB of HBM per device.

v0:
```python
import jax
import jax.numpy as jnp
from jax import lax
from jax.sharding import PartitionSpec as P

LAGS = 256


def passed_along(value, axis, steps):
    count = lax.axis_size(axis)
    first, last = (max(0, -steps), min(count, count - steps))
    return lax.ppermute(value, axis, [(source, source + steps) for source in range(first, last)])


def from_everyone(array, axis):
    devices = lax.axis_size(axis)
    return lax.all_to_all(
        jnp.broadcast_to(array[None], (devices, *array.shape)), axis, 0, 0, tiled=True
    )


def taken_together(array, axis):
    return from_everyone(array, axis).sum(axis=0)


def packed_total(arrays, axis):
    line, at, gathered = (jnp.concatenate([a.reshape(-1) for a in arrays]), 0, [])
    running = taken_together(line, axis)
    for a in arrays:
        gathered.append(running[at : at + a.size].reshape(a.shape))
        at += a.size
    return tuple(gathered)


def body(velocities, atom_mask, valid_frames):
    frame_count, xyz_count, atom_count = velocities.shape
    last_valid = valid_frames[0]
    anchor_frame = lax.axis_index("tm") * frame_count
    in_range = anchor_frame + jnp.arange(frame_count, dtype=jnp.int32) < last_valid
    clean = jnp.where(in_range[:, None, None], velocities, jnp.zeros_like(velocities))
    leading = clean[: LAGS - 1]
    following = passed_along(leading, "tm", -1)
    extended = jnp.concatenate(
        [clean, following, jnp.zeros((1, xyz_count, atom_count), clean.dtype)], 0
    )
    lag_group = 16
    clean_wide = clean.astype(jnp.float32)

    def block(block_index, lag_sums):
        for member in range(lag_group):
            offset = block_index * lag_group + member
            shifted = lax.dynamic_slice_in_dim(extended, offset, frame_count, 0)
            row_sum = jnp.sum(clean_wide * shifted.astype(jnp.float32), axis=(0, 1))
            lag_sums = lax.dynamic_update_slice_in_dim(lag_sums, row_sum[None, :], offset, 0)
        return lag_sums

    lag_sums = lax.fori_loop(
        0, LAGS // lag_group, block, jnp.zeros((LAGS, atom_count), jnp.float32)
    )
    per_device = LAGS // lax.axis_size("tm")
    first_lag = lax.axis_index("tm") * per_device
    own_rows = lax.psum_scatter(lag_sums, "tm", scatter_dimension=0, tiled=True)
    lag_index = first_lag + jnp.arange(per_device, dtype=jnp.int32)
    anchors = (last_valid - lag_index).astype(jnp.float32)
    atom_weight = atom_mask.astype(jnp.float32)
    correlation = atom_weight[None, :] * own_rows / anchors[:, None]
    total_corr, real_atoms = packed_total(
        (jnp.sum(correlation, axis=1), jnp.sum(atom_weight)), "comp"
    )
    average = total_corr / jnp.maximum(real_atoms, 1.0)
    return (correlation, average)


def solution(mesh):
    return jax.shard_map(
        body,
        mesh=mesh,
        in_specs=(P("tm", None, "comp"), P("comp"), P()),
        out_specs=(P("tm", "comp"), P("tm")),
        check_vma=False,
    )
```

profile of v0, /device:TPU:1, one launch (start us, length us, event | category | flops | bytes accessed | tf_op | source)
XLA Modules:
  0.0 356.3 jit_solution(2404851723241863948)
XLA Ops:
  9.1 5.1 %collective-permute-start = (bf16[255,3,512]{2,0,1:T(8,128)(2,1)S(1)}, bf16[255,3,512]{2,0,1:T(8,128)(2,1)S(1)}, u32[]{:S(2)}, u32[]{:S(2)}) collective-permute-start(bf16[255,3,512]{2,0,1:T(8,128)(2,1)S(1)} %bitcast.56), channel_id=1, source_target_pairs={{8,0},{16,8},{24,16},{32,24},{40,32},{48,40},{56,48},{64,56},{72,6... | collective-permute-start | bytes 2350088 | tf_op jit(solution)/shard_map/ppermute | solution.py:12
  14.3 2.0 copy.11
  16.4 8.4 %collective-permute-done = bf16[255,3,512]{2,0,1:T(8,128)(2,1)S(1)} collective-permute-done((bf16[255,3,512]{2,0,1:T(8,128)(2,1)S(1)}, bf16[255,3,512]{2,0,1:T(8,128)(2,1)S(1)}, u32[]{:S(2)}, u32[]{:S(2)}) %collective-permute-start) | collective-permute-done | bytes 783392 | tf_op jit(solution)/shard_map/ppermute | solution.py:12
  25.2 1.4 copy.10
  26.6 197.5 %while.15 = (s32[]{:T(128)}, f32[256,512]{1,0:T(8,128)S(1)}, bf16[512,3,512]{2,1,0:T(4,128)(2,1)S(1)}, f32[256,3,512]{2,1,0:T(4,128)}, s32[]{:T(128)}, /*index=5...) while((s32[]{:T(128)}, f32[256,512]{1,0:T(8,128)S(1)}, ...), condition=%wide.region_17.18_spmd, body=%wide.region_0.17_spmd.sunk | while | flops 18866240 | bytes 14255789 | solution.py:57
  26.7 11.0 %multiply_reduce_fusion.17 = (f32[512]{0:T(512)S(1)}, f32[512]{0:T(512)S(1)}, f32[512]{0:T(512)S(1)}, f32[512]{0:T(512)S(1)}, f32[512]{0:T(512)S(1)}, /*index=5*...) fusion(f32[256,3,512]{2,1,0:T(4,128)} %get-tuple-element.346, ...), kind=kLoop, calls=%fused_computation.clone.1 | loop fusion | flops 18866176 | bytes 14188608 | tf_op jit(solution)/shard_map/while/body/eval_jaxpr/reduce_sum | solution.py:53
  39.1 11.0 %multiply_reduce_fusion.17 = (f32[512]{0:T(512)S(1)}, f32[512]{0:T(512)S(1)}, f32[512]{0:T(512)S(1)}, f32[512]{0:T(512)S(1)}, f32[512]{0:T(512)S(1)}, /*index=5*...) fusion(f32[256,3,512]{2,1,0:T(4,128)} %get-tuple-element.346, ...), kind=kLoop, calls=%fused_computation.clone.1 | loop fusion | flops 18866176 | bytes 14188608 | tf_op jit(solution)/shard_map/while/body/eval_jaxpr/reduce_sum | solution.py:53
  51.4 11.0 %multiply_reduce_fusion.17 = (f32[512]{0:T(512)S(1)}, f32[512]{0:T(512)S(1)}, f32[512]{0:T(512)S(1)}, f32[512]{0:T(512)S(1)}, f32[512]{0:T(512)S(1)}, /*index=5*...) fusion(f32[256,3,512]{2,1,0:T(4,128)} %get-tuple-element.346, ...), kind=kLoop, calls=%fused_computation.clone.1 | loop fusion | flops 18866176 | bytes 14188608 | tf_op jit(solution)/shard_map/while/body/eval_jaxpr/reduce_sum | solution.py:53
  63.8 11.0 %multiply_reduce_fusion.17 = (f32[512]{0:T(512)S(1)}, f32[512]{0:T(512)S(1)}, f32[512]{0:T(512)S(1)}, f32[512]{0:T(512)S(1)}, f32[512]{0:T(512)S(1)}, /*index=5*...) fusion(f32[256,3,512]{2,1,0:T(4,128)} %get-tuple-element.346, ...), kind=kLoop, calls=%fused_computation.clone.1 | loop fusion | flops 18866176 | bytes 14188608 | tf_op jit(solution)/shard_map/while/body/eval_jaxpr/reduce_sum | solution.py:53
  76.1 11.0 %multiply_reduce_fusion.17 = (f32[512]{0:T(512)S(1)}, f32[512]{0:T(512)S(1)}, f32[512]{0:T(512)S(1)}, f32[512]{0:T(512)S(1)}, f32[512]{0:T(512)S(1)}, /*index=5*...) fusion(f32[256,3,512]{2,1,0:T(4,128)} %get-tuple-element.346, ...), kind=kLoop, calls=%fused_computation.clone.1 | loop fusion | flops 18866176 | bytes 14188608 | tf_op jit(solution)/shard_map/while/body/eval_jaxpr/reduce_sum | solution.py:53
  88.5 11.0 %multiply_reduce_fusion.17 = (f32[512]{0:T(512)S(1)}, f32[512]{0:T(512)S(1)}, f32[512]{0:T(512)S(1)}, f32[512]{0:T(512)S(1)}, f32[512]{0:T(512)S(1)}, /*index=5*...) fusion(f32[256,3,512]{2,1,0:T(4,128)} %get-tuple-element.346, ...), kind=kLoop, calls=%fused_computation.clone.1 | loop fusion | flops 18866176 | bytes 14188608 | tf_op jit(solution)/shard_map/while/body/eval_jaxpr/reduce_sum | solution.py:53
  100.8 11.0 %multiply_reduce_fusion.17 = (f32[512]{0:T(512)S(1)}, f32[512]{0:T(512)S(1)}, f32[512]{0:T(512)S(1)}, f32[512]{0:T(512)S(1)}, f32[512]{0:T(512)S(1)}, /*index=5*...) fusion(f32[256,3,512]{2,1,0:T(4,128)} %get-tuple-element.346, ...), kind=kLoop, calls=%fused_computation.clone.1 | loop fusion | flops 18866176 | bytes 14188608 | tf_op jit(solution)/shard_map/while/body/eval_jaxpr/reduce_sum | solution.py:53
  113.1 11.0 %multiply_reduce_fusion.17 = (f32[512]{0:T(512)S(1)}, f32[512]{0:T(512)S(1)}, f32[512]{0:T(512)S(1)}, f32[512]{0:T(512)S(1)}, f32[512]{0:T(512)S(1)}, /*index=5*...) fusion(f32[256,3,512]{2,1,0:T(4,128)} %get-tuple-element.346, ...), kind=kLoop, calls=%fused_computation.clone.1 | loop fusion | flops 18866176 | bytes 14188608 | tf_op jit(solution)/shard_map/while/body/eval_jaxpr/reduce_sum | solution.py:53
  125.5 11.0 %multiply_reduce_fusion.17 = (f32[512]{0:T(512)S(1)}, f32[512]{0:T(512)S(1)}, f32[512]{0:T(512)S(1)}, f32[512]{0:T(512)S(1)}, f32[512]{0:T(512)S(1)}, /*index=5*...) fusion(f32[256,3,512]{2,1,0:T(4,128)} %get-tuple-element.346, ...), kind=kLoop, calls=%fused_computation.clone.1 | loop fusion | flops 18866176 | bytes 14188608 | tf_op jit(solution)/shard_map/while/body/eval_jaxpr/reduce_sum | solution.py:53
  137.8 11.0 %multiply_reduce_fusion.17 = (f32[512]{0:T(512)S(1)}, f32[512]{0:T(512)S(1)}, f32[512]{0:T(512)S(1)}, f32[512]{0:T(512)S(1)}, f32[512]{0:T(512)S(1)}, /*index=5*...) fusion(f32[256,3,512]{2,1,0:T(4,128)} %get-tuple-element.346, ...), kind=kLoop, calls=%fused_computation.clone.1 | loop fusion | flops 18866176 | bytes 14188608 | tf_op jit(solution)/shard_map/while/body/eval_jaxpr/reduce_sum | solution.py:53
  150.2 11.0 %multiply_reduce_fusion.17 = (f32[512]{0:T(512)S(1)}, f32[512]{0:T(512)S(1)}, f32[512]{0:T(512)S(1)}, f32[512]{0:T(512)S(1)}, f32[512]{0:T(512)S(1)}, /*index=5*...) fusion(f32[256,3,512]{2,1,0:T(4,128)} %get-tuple-element.346, ...), kind=kLoop, calls=%fused_computation.clone.1 | loop fusion | flops 18866176 | bytes 14188608 | tf_op jit(solution)/shard_map/while/body/eval_jaxpr/reduce_sum | solution.py:53
  162.5 11.0 %multiply_reduce_fusion.17 = (f32[512]{0:T(512)S(1)}, f32[512]{0:T(512)S(1)}, f32[512]{0:T(512)S(1)}, f32[512]{0:T(512)S(1)}, f32[512]{0:T(512)S(1)}, /*index=5*...) fusion(f32[256,3,512]{2,1,0:T(4,128)} %get-tuple-element.346, ...), kind=kLoop, calls=%fused_computation.clone.1 | loop fusion | flops 18866176 | bytes 14188608 | tf_op jit(solution)/shard_map/while/body/eval_jaxpr/reduce_sum | solution.py:53
  174.9 11.0 %multiply_reduce_fusion.17 = (f32[512]{0:T(512)S(1)}, f32[512]{0:T(512)S(1)}, f32[512]{0:T(512)S(1)}, f32[512]{0:T(512)S(1)}, f32[512]{0:T(512)S(1)}, /*index=5*...) fusion(f32[256,3,512]{2,1,0:T(4,128)} %get-tuple-element.346, ...), kind=kLoop, calls=%fused_computation.clone.1 | loop fusion | flops 18866176 | bytes 14188608 | tf_op jit(solution)/shard_map/while/body/eval_jaxpr/reduce_sum | solution.py:53
  187.2 11.0 %multiply_reduce_fusion.17 = (f32[512]{0:T(512)S(1)}, f32[512]{0:T(512)S(1)}, f32[512]{0:T(512)S(1)}, f32[512]{0:T(512)S(1)}, f32[512]{0:T(512)S(1)}, /*index=5*...) fusion(f32[256,3,512]{2,1,0:T(4,128)} %get-tuple-element.346, ...), kind=kLoop, calls=%fused_computation.clone.1 | loop fusion | flops 18866176 | bytes 14188608 | tf_op jit(solution)/shard_map/while/body/eval_jaxpr/reduce_sum | solution.py:53
  199.6 11.0 %multiply_reduce_fusion.17 = (f32[512]{0:T(512)S(1)}, f32[512]{0:T(512)S(1)}, f32[512]{0:T(512)S(1)}, f32[512]{0:T(512)S(1)}, f32[512]{0:T(512)S(1)}, /*index=5*...) fusion(f32[256,3,512]{2,1,0:T(4,128)} %get-tuple-element.346, ...), kind=kLoop, calls=%fused_computation.clone.1 | loop fusion | flops 18866176 | bytes 14188608 | tf_op jit(solution)/shard_map/while/body/eval_jaxpr/reduce_sum | solution.py:53
  211.9 11.0 %multiply_reduce_fusion.17 = (f32[512]{0:T(512)S(1)}, f32[512]{0:T(512)S(1)}, f32[512]{0:T(512)S(1)}, f32[512]{0:T(512)S(1)}, f32[512]{0:T(512)S(1)}, /*index=5*...) fusion(f32[256,3,512]{2,1,0:T(4,128)} %get-tuple-element.346, ...), kind=kLoop, calls=%fused_computation.clone.1 | loop fusion | flops 18866176 | bytes 14188608 | tf_op jit(solution)/shard_map/while/body/eval_jaxpr/reduce_sum | solution.py:53
  225.6 111.1 %reduce-scatter.2.cloned.1.call-done = f32[8,512]{1,0:T(8,128)} async-done(((f32[256,512]{1,0:T(8,128)}), f32[8,512]{1,0:T(8,128)}) %reduce-scatter.2.cloned.1.call-update) | async-done | bytes 16400 | tf_op jit(solution)/shard_map/reduce_scatter | solution.py:62
  336.6 1.5 fusion
  338.9 8.8 %all_to_all.6 = f32[8,1,9]{2,1,0:T(1,128)S(1)} all-to-all(f32[8,1,9]{2,1,0:T(1,128)S(1)} %broadcast_in_dim.190), channel_id=1, replica_groups=mesh['tm'=32,'comp'=8] {'comp'}, dimensions={0} | all-to-all | bytes 576 | tf_op jit(solution)/shard_map/all_to_all | solution.py:17
  (275 shorter events, 20.6 us)
Async XLA Ops:
  7.2 329.5 %reduce-scatter.2.cloned.1.call-start = ((), (), s32[]{:S(2)}) async-start(), calls=%async_computation.2 | async-start | bytes 540672 | tf_op jit(solution)/shard_map/reduce_scatter | solution.py:62
  9.1 15.7 %collective-permute-start = (bf16[255,3,512]{2,0,1:T(8,128)(2,1)S(1)}, bf16[255,3,512]{2,0,1:T(8,128)(2,1)S(1)}, u32[]{:S(2)}, u32[]{:S(2)}) collective-permute-start(bf16[255,3,512]{2,0,1:T(8,128)(2,1)S(1)} %bitcast.56), channel_id=1, source_target_pairs={{8,0},{16,8},{24,16},{32,24},{40,32},{48,40},{56,48},{64,56},{72,6... | collective-permute-start | bytes 2350088 | tf_op jit(solution)/shard_map/ppermute | solution.py:12
  26.6 198.3 %copy-start.1 = (s32[512]{0:T(512)S(1)}, s32[512]{0:T(512)}, u32[]{:S(2)}) copy-start(s32[512]{0:T(512)} %param.6) | copy-start | bytes 6148
  224.1 0.8 copy-start
Sparse Core Ops, SparseCore 0:
  225.1 111.5 reduce-scatter.1
where the time goes:
time: 362 us; the launch traced here: 356 us
  other arithmetic  180 us (50%)
  waiting for transfers between devices  120 us (33%)
  local copies, waits for them, and re-layouts  20.5 us (6%)
  between operations  15.4 us (4%)
  blocking collectives  8.81 us (2%)
  loops' own time  6.67 us (2%)
  starting transfers between devices  5.19 us (1%)
    reduce_sum x16, other arithmetic, block(): row_sum = jnp.sum(clean_wide * shifted.astype(jnp.float32), axis=(0, 1))  175 us
    reduce_scatter x1, waiting for transfers between devices, body(): own_rows = lax.psum_scatter(lag_sums, 'tm', scatter_dimension=0, tiled=True)  111 us
    dynamic_update_slice x256, local copies, waits for them, and re-layouts, block(): lax.dynamic_update_slice_in_dim(lag_sums, row_sum[None, :], offset, 0)  15.6 us
    all_to_all x1, blocking collectives, from_everyone(): lax.all_to_all(jnp.broadcast_to(array[None], (devices, *array.shape)), ax...  8.81 us
    ppermute x1, waiting for transfers between devices, passed_along(): lax.ppermute(value, axis, [(source, source + steps) for source in range(f...  8.45 us
  transfers between devices with their start and end apart: 2, of which 2 were waited for; matrix products, arithmetic and copies ran while one was open for 1% of the time, Pallas kernels for 0%

commit v1 on v0

v1 whole, which is shorter than its diff:
```python
import jax
import jax.numpy as jnp
import ml_dtypes
import numpy as np
from jax import lax
from jax.experimental import pallas as pl
from jax.experimental.pallas import tpu as pltpu
from jax.sharding import PartitionSpec as P

LAGS = 256
FRAMES = 256
SIZE = 512
LANES = 128
GROUP = 4


def two_parts(table):
    high = table.astype(ml_dtypes.bfloat16)
    low = (table - high.astype(np.float64)).astype(ml_dtypes.bfloat16)
    return high, low


def tables():
    f = np.concatenate([np.arange(0, SIZE // 2, 2), np.arange(1, SIZE // 2, 2)])
    angle = 2.0 * np.pi * (f + 0.5) / SIZE
    ahead = angle[:, None] * np.arange(FRAMES)[None, :]
    forward = np.concatenate([np.cos(ahead), -np.sin(ahead)], 0)
    back = angle[None, :] * np.arange(LAGS)[:, None]
    inverse = np.concatenate([np.cos(back), -np.sin(back)], 1) * (2.0 / SIZE)
    return two_parts(forward), two_parts(inverse)


def dot(a, b):
    return jnp.dot(a, b, preferred_element_type=jnp.float32)


def lag_kernel(valid_ref, own, core, across, corner, near, fh, fl, ih, il, out, spec, power):
    tm = lax.axis_index("tm")
    z, q = tm // GROUP, tm % GROUP
    lower = q < 2
    valid = valid_ref[0]
    frame = lax.broadcasted_iota(jnp.int32, (FRAMES, LANES), 0)

    def transform(ref, slot, block):
        keep = frame + block * FRAMES < valid
        part = [
            jnp.where(keep, ref[k].astype(jnp.float32), 0.0).astype(jnp.bfloat16)
            for k in range(3)
        ]
        clean = jnp.concatenate(part, axis=1)
        spec[slot] = dot(fh[...], clean) + dot(fl[...], clean)

    base = z * GROUP
    transform(own, q, base + q)
    transform(core, q ^ 1, base + (q ^ 1))
    transform(near, GROUP, jnp.where(lower, base + GROUP, base - 1))
    transform(across, q ^ 2, base + (q ^ 2))
    transform(corner, q ^ 3, base + (q ^ 3))

    first = jnp.where(lower, 3, 4)
    second = jnp.where(lower, 4, 0)
    half = SIZE // 2
    rows = 8
    for parity in range(2):

        def step(r, carry):
            at = pl.multiple_of(parity * (half // 2) + r * rows, rows)
            re = lambda j: spec[j, pl.ds(at, rows), :]
            im = lambda j: spec[j, pl.ds(half + at, rows), :]
            a = [(re(j), im(j)) for j in range(GROUP)]
            same = sum(x * x + y * y for x, y in a)
            pairs = [(a[0], a[1]), (a[1], a[2]), (a[2], a[3])]
            pairs.append(((re(first), im(first)), (re(second), im(second))))
            cr = sum(x[0] * y[1] - x[1] * y[0] for x, y in pairs)
            ci = sum(x[0] * y[0] + x[1] * y[1] for x, y in pairs)
            pr = same + cr if parity == 0 else same - cr
            pi = -ci if parity == 0 else ci
            fold = lambda t: t[:, :LANES] + t[:, LANES : 2 * LANES] + t[:, 2 * LANES :]
            power[pl.ds(at, rows), :] = fold(pr)
            power[pl.ds(half + at, rows), :] = fold(pi)
            return carry

        lax.fori_loop(0, half // 2 // rows, step, 0)

    p = power[...]
    ph = p.astype(jnp.bfloat16)
    pl_ = (p - ph.astype(jnp.float32)).astype(jnp.bfloat16)
    out[...] = dot(ih[...], ph) + (dot(il[...], ph) + dot(ih[...], pl_))


def lag_sums_of(valid_frames, pieces):
    (fh, fl), (ih, il) = tables()
    vmem = pl.BlockSpec(memory_space=pltpu.VMEM)
    smem = pl.BlockSpec(memory_space=pltpu.SMEM)
    return pl.pallas_call(
        lag_kernel,
        out_shape=jax.ShapeDtypeStruct((LAGS, LANES), jnp.float32),
        in_specs=[smem] + [vmem] * 9,
        out_specs=vmem,
        scratch_shapes=[
            pltpu.VMEM((GROUP + 1, SIZE, 3 * LANES), jnp.float32),
            pltpu.VMEM((SIZE, LANES), jnp.float32),
        ],
        compiler_params=pltpu.CompilerParams(vmem_limit_bytes=32 * 1024 * 1024),
        name="lag_sums",
    )(valid_frames, *pieces, fh, fl, ih, il)


def finish_kernel(valid_ref, mask_ref, parts, corr, sums):
    tm = lax.axis_index("tm")
    per = corr.shape[0]
    lag = tm * per + lax.broadcasted_iota(jnp.int32, (per, LANES), 0)
    anchors = (valid_ref[0] - lag).astype(jnp.float32)
    total = jnp.zeros((per, LANES), jnp.float32)
    count = jnp.zeros((1, LANES), jnp.float32)
    for q in range(GROUP):
        lanes = slice(q * LANES, (q + 1) * LANES)
        lag_sum = parts[q]
        for z in range(1, parts.shape[0] // GROUP):
            lag_sum = lag_sum + parts[z * GROUP + q]
        weight = mask_ref[:, lanes].astype(jnp.float32)
        value = weight * lag_sum / anchors
        corr[:, lanes] = value
        total = total + value
        count = count + weight
    row = jnp.sum(total, axis=1, keepdims=True)
    real = jnp.sum(count, axis=1, keepdims=True)
    lane = lax.broadcasted_iota(jnp.int32, (per, LANES), 1)
    line = jnp.where(lane < LANES // 2, row, real)
    sums[...] = jnp.broadcast_to(line[None], sums.shape)


def body(velocities, atom_mask, valid_frames):
    count = lax.axis_size("tm")
    q = lax.axis_index("tm") % GROUP
    by_axis = velocities.transpose(1, 0, 2)

    def piece(k):
        return lax.dynamic_slice(by_axis, (0, 0, (q ^ k) * LANES), (3, FRAMES, LANES))

    def swapped(k):
        return lax.ppermute(piece(k), "tm", [(s, s ^ k) for s in range(count)])

    own, across, corner, core = piece(0), swapped(2), swapped(3), swapped(1)
    edge = jnp.where((q == 0) | (q == 3), own, core)
    hops = [(s, s - GROUP if s % GROUP < 2 else s + GROUP) for s in range(count)]
    near = lax.ppermute(edge, "tm", [(s, d) for s, d in hops if 0 <= d < count])

    lag_sums = lag_sums_of(valid_frames, (own, core, across, corner, near))
    per = LAGS // count
    parts = lax.all_to_all(
        lag_sums.reshape(count, per, LANES), "tm", 0, 0, tiled=True
    )
    atoms = atom_mask.shape[0]
    comps = lax.axis_size("comp")
    vmem = pl.BlockSpec(memory_space=pltpu.VMEM)
    correlation, sums = pl.pallas_call(
        finish_kernel,
        out_shape=(
            jax.ShapeDtypeStruct((per, atoms), jnp.float32),
            jax.ShapeDtypeStruct((comps, per, LANES), jnp.float32),
        ),
        in_specs=[pl.BlockSpec(memory_space=pltpu.SMEM), vmem, vmem],
        out_specs=(vmem, vmem),
        name="finish",
    )(valid_frames, atom_mask.reshape(1, atoms), parts)
    everyone = lax.all_to_all(sums, "comp", 0, 0, tiled=True).sum(0)
    average = everyone[:, 0] / jnp.maximum(everyone[:, LANES // 2], 1.0)
    return correlation, average


def solution(mesh):
    return jax.shard_map(
        body,
        mesh=mesh,
        in_specs=(P("tm", None, "comp"), P("comp"), P()),
        out_specs=(P("tm", "comp"), P("tm")),
        check_vma=False,
    )
```

time: 362 us -> 54.7 us (0.15); the launches traced: 356 us -> 54.4 us
  other arithmetic: 180 us -> 1.78 us
  waiting for transfers between devices: 120 us -> 6.3 us
  blocking collectives: 8.81 us -> 31.5 us
  local copies, waits for them, and re-layouts: 20.5 us -> 1.23 us
  between operations: 15.4 us -> 1.36 us
  loops' own time: 6.67 us -> 0 us
  Pallas kernels: 0 us -> 4.4 us
    reduce_sum x19 -> x1, other arithmetic: 177 us -> 0.01 us  [body(): everyone = lax.all_to_all(sums, 'comp', 0, 0, tiled=True).sum(0)]
    reduce_scatter x1 -> x0, waiting for transfers between devices: 111 us -> none  [body(): own_rows = lax.psum_scatter(lag_sums, 'tm', scatter_dimension=0, tiled=True)]
    all_to_all x1 -> x2, blocking collectives: 8.81 us -> 31.5 us  [the longest x1 22.2 us: body(): lax.all_to_all(lag_sums.reshape(count, per, LANES), 'tm', 0, 0, tiled=True)]
    dynamic_update_slice x256 -> x0, local copies, waits for them, and re-layouts: 15.6 us -> none  [block(): lax.dynamic_update_slice_in_dim(lag_sums, row_sum[None, :], offset, 0)]
    another operation x1 -> x0, loops' own time: 6.67 us -> none  [body(): lax.fori_loop(0, LAGS // lag_group, block, jnp.zeros((LAGS, atom_count),...]
    pallas_call x0 -> x2, Pallas kernels: none -> 4.4 us  [the longest x1 2.78 us: lag_sums_of(): pl.pallas_call(lag_kernel, out_shape=jax.ShapeDtypeStruct((LAGS, LANES),...]
    ppermute x1 -> x4, starting transfers between devices: 5.15 us -> 7.85 us  [the longest x3 6.56 us: swapped(): return lax.ppermute(piece(k), 'tm', [(s, s ^ k) for s in range(count)])]
    ppermute x1 -> x4, waiting for transfers between devices: 8.45 us -> 6.3 us  [the longest x3 6.1 us: swapped(): return lax.ppermute(piece(k), 'tm', [(s, s ^ k) for s in range(count)])]
  transfers between devices with their start and end apart: 2 -> 4, of which waited for: 2 -> 3; matrix products, arithmetic and copies ran while one was open for 1% -> 2% of each run, Pallas kernels for 0% -> 0%
where the time goes in v1:
time: 54.7 us; the launch traced here: 54.4 us
  blocking collectives  31.5 us (58%)
  starting transfers between devices  7.85 us (14%)
  waiting for transfers between devices  6.3 us (12%)
  Pallas kernels  4.4 us (8%)
  other arithmetic  1.78 us (3%)
  between operations  1.36 us (2%)
  local copies, waits for them, and re-layouts  1.23 us (2%)
    all_to_all x1, blocking collectives, body(): lax.all_to_all(lag_sums.reshape(count, per, LANES), 'tm', 0, 0, tiled=True)  22.2 us
    all_to_all x1, blocking collectives, body(): everyone = lax.all_to_all(sums, 'comp', 0, 0, tiled=True).sum(0)  9.33 us
    ppermute x3, starting transfers between devices, swapped(): return lax.ppermute(piece(k), 'tm', [(s, s ^ k) for s in range(count)])  6.56 us
    ppermute x3, waiting for transfers between devices, swapped(): return lax.ppermute(piece(k), 'tm', [(s, s ^ k) for s in range(count)])  6.1 us
    pallas_call x1, Pallas kernels, lag_sums_of(): pl.pallas_call(lag_kernel, out_shape=jax.ShapeDtypeStruct((LAGS, LANES),...  2.78 us
    pallas_call x1, Pallas kernels, body(): pl.pallas_call(finish_kernel, out_shape=(jax.ShapeDtypeStruct((per, atoms...  1.63 us
    ppermute x1, starting transfers between devices, body(): near = lax.ppermute(edge, 'tm', [(s, d) for s, d in hops if 0 <= d < count])  1.29 us
    dynamic_slice x1, local copies, waits for them, and re-layouts, piece(): lax.dynamic_slice(by_axis, (0, 0, (q ^ k) * LANES), (3, FRAMES, LANES))  1.22 us
  transfers between devices with their start and end apart: 4, of which 3 were waited for; matrix products, arithmetic and copies ran while one was open for 2% of the time, Pallas kernels for 0%

profile of v1, /device:TPU:1, one launch (start us, length us, event | category | flops | bytes accessed | tf_op | source)
XLA Modules:
  0.0 54.4 jit_solution(7136573332112422739)
XLA Ops:
  0.7 0.0 copy-start.3
  0.7 1.2 %dynamic-slice_bitcast_fusion = (bf16[3,256,128]{2,1,0:T(8,128)(2,1)S(1)}, bf16[3,256,128]{2,1,0:T(8,128)(2,1)S(1)}, bf16[3,256,128]{2,1,0:T(8,128)(2,1)S(1)}) fusion(bf16[256,3,512]{2,0,1:T(8,128)(2,1)} %param.7, s32[]{:T(128)S(6)} %select_n.31, s32[]{:T(128)S(6)} %select_n.29, s32[]{:T(128)S(6)} %select_n.30), kind=kLoop, calls=%fused_computation | loop fusion | bytes 1179660 | tf_op jit(solution)/shard_map/dynamic_slice | solution.py:139
  1.9 3.3 %collective-permute-start = (bf16[3,256,128]{2,1,0:T(8,128)(2,1)S(1)}, bf16[3,256,128]{2,1,0:T(8,128)(2,1)S(1)}, u32[]{:S(2)}, u32[]{:S(2)}) collective-permute-start(bf16[3,256,128]{2,1,0:T(8,128)(2,1)S(1)} %get-tuple-element.9), channel_id=1, source_target_pairs={{0,8},{8,0},{16,24},{24,16},{32,40},{40,32},{48,56},{56,48},{64,72... | collective-permute-start | bytes 589832 | tf_op jit(solution)/shard_map/ppermute | solution.py:142
  5.2 1.0 %collective-permute-start.1 = (bf16[3,256,128]{2,1,0:T(8,128)(2,1)S(1)}, bf16[3,256,128]{2,1,0:T(8,128)(2,1)S(1)}, u32[]{:S(2)}, u32[]{:S(2)}) collective-permute-start(bf16[3,256,128]{2,1,0:T(8,128)(2,1)S(1)} %get-tuple-element.10), channel_id=1, source_target_pairs={{0,16},{8,24},{16,0},{24,8},{32,48},{40,56},{48,32},{56,40},{64,80... | collective-permute-start | bytes 589832 | tf_op jit(solution)/shard_map/ppermute | solution.py:142
  6.2 2.2 %collective-permute-start.2 = (bf16[3,256,128]{2,1,0:T(8,128)(2,1)S(1)}, bf16[3,256,128]{2,1,0:T(8,128)(2,1)S(1)}, u32[]{:S(2)}, u32[]{:S(2)}) collective-permute-start(bf16[3,256,128]{2,1,0:T(8,128)(2,1)S(1)} %get-tuple-element.8), channel_id=1, source_target_pairs={{0,24},{8,16},{16,8},{24,0},{32,56},{40,48},{48,40},{56,32},{64,88... | collective-permute-start | bytes 589832 | tf_op jit(solution)/shard_map/ppermute | solution.py:142
  8.5 0.0 copy-start
  8.5 0.0 copy-start.1
  8.5 0.0 copy-start.2
  8.5 0.0 collective-permute-done.core
  8.5 1.1 %broadcast_select_fusion = (bf16[3,256,128]{2,1,0:T(8,128)(2,1)S(1)}, bf16[3,256,128]{2,1,0:T(8,128)(2,1)S(1)}) fusion(bf16[3,256,128]{2,1,0:T(8,128)(2,1)S(1)} %collective-permute-done.core, pred[]{:T(512)S(6)} %or.3, bf16[256,3,512]{2,0,1:T(8,128)(2,1)} %param.7, s32[]{:T(128)S(6)} %select_n.28), kind=kLoop, calls=%fused_computation.4 | loop fusion | flops 98304 | bytes 786437 | tf_op jit(solution)/shard_map/jit(_where)/select_n | solution.py:145
  9.5 1.3 %collective-permute-start.3 = (bf16[3,256,128]{2,1,0:T(8,128)(2,1)S(1)}, bf16[3,256,128]{2,1,0:T(8,128)(2,1)S(1)}, u32[]{:S(2)}, u32[]{:S(2)}) collective-permute-start(bf16[3,256,128]{2,1,0:T(8,128)(2,1)S(1)} %get-tuple-element.6), channel_id=1, source_target_pairs={{16,48},{24,56},{32,0},{40,8},{48,80},{56,88},{64,32},{72,40},{80,... | collective-permute-start | bytes 589832 | tf_op jit(solution)/shard_map/ppermute | solution.py:147
  11.5 1.7 %collective-permute-done.1.across = bf16[3,256,128]{2,1,0:T(8,128)(2,1)S(1)} collective-permute-done((bf16[3,256,128]{2,1,0:T(8,128)(2,1)S(1)}, bf16[3,256,128]{2,1,0:T(8,128)(2,1)S(1)}, u32[]{:S(2)}, u32[]{:S(2)}) %collective-permute-start.1) | collective-permute-done | bytes 196640 | tf_op jit(solution)/shard_map/ppermute | solution.py:142
  13.2 4.4 %collective-permute-done.2.corner = bf16[3,256,128]{2,1,0:T(8,128)(2,1)S(1)} collective-permute-done((bf16[3,256,128]{2,1,0:T(8,128)(2,1)S(1)}, bf16[3,256,128]{2,1,0:T(8,128)(2,1)S(1)}, u32[]{:S(2)}, u32[]{:S(2)}) %collective-permute-start.2) | collective-permute-done | bytes 196640 | tf_op jit(solution)/shard_map/ppermute | solution.py:142
  17.6 0.2 collective-permute-done.3.near
  17.8 0.0 copy-done.3
  17.8 0.0 copy-done
  17.8 0.0 copy-done.1
  17.8 0.0 copy-done.2
  17.8 2.8 %lag_sums.1 = f32[256,128]{1,0:T(8,128)S(1)} custom-call(s32[1]{0:T(128)S(6)} %copy.9.valid_ref, bf16[3,256,128]{2,1,0:T(8,128)(2,1)S(1)} %get-tuple-element.7.own, bf16[3,256,128]{2,1,0:T(8,128)(2,1)S(1)} %collective-permute-done.core, bf16[3,256,128]{2,1,0:T(8,128)(2,1)S(1)} %collective-permute-done.1.across, ...), custom_call_target="tpu_custom_call" | custom-call | tf_op jit(solution)/shard_map/lag_sums/pallas_call | solution.py:95
  20.6 22.2 %all_to_all.10.parts = f32[32,8,128]{2,1,0:T(8,128)} all-to-all(f32[32,8,128]{2,1,0:T(8,128)S(1)} %bitcast.11), channel_id=1, replica_groups=mesh['tm'=32,'comp'=8] {'tm'}, dimensions={0} | all-to-all | bytes 262144 | tf_op jit(solution)/shard_map/all_to_all | solution.py:151
  42.8 1.6 %finish.1 = (f32[8,512]{1,0:T(8,128)}, f32[8,8,128]{2,1,0:T(8,128)}) custom-call(s32[1]{0:T(128)S(6)} %copy.9.valid_ref, s32[1,512]{1,0:T(1,128)} %bitcast.12, f32[32,8,128]{2,1,0:T(8,128)} %all_to_all.10.parts), custom_call_target="tpu_custom_call" | custom-call | tf_op jit(solution)/shard_map/finish/pallas_call | solution.py:157
  44.4 9.3 %all_to_all.11 = f32[8,8,128]{2,1,0:T(8,128)S(1)} all-to-all(f32[8,8,128]{2,1,0:T(8,128)} %get-tuple-element.5), channel_id=1, replica_groups=mesh['tm'=32,'comp'=8] {'comp'}, dimensions={0} | all-to-all | bytes 65536 | tf_op jit(solution)/shard_map/all_to_all | solution.py:167
  53.7 0.7 %divide_reduce_fusion = f32[8]{0:T(128)} fusion(f32[8,128]{1,0:T(8,128)S(1)} %reduce_sum.9), kind=kLoop, calls=%fused_computation.5 | loop fusion | flops 16 | bytes 96 | tf_op jit(solution)/shard_map/div | solution.py:168
  (1 shorter events, 0.0 us)
Async XLA Ops:
  0.7 17.1 %copy-start.3 = (bf16[256,512]{1,0:T(8,128)(2,1)S(1)}, bf16[256,512]{1,0:T(8,128)(2,1)}, u32[]{:S(2)}) copy-start(bf16[256,512]{1,0:T(8,128)(2,1)} %constant.44.clone.il) | copy-start | bytes 786436
  1.9 6.6 %collective-permute-start = (bf16[3,256,128]{2,1,0:T(8,128)(2,1)S(1)}, bf16[3,256,128]{2,1,0:T(8,128)(2,1)S(1)}, u32[]{:S(2)}, u32[]{:S(2)}) collective-permute-start(bf16[3,256,128]{2,1,0:T(8,128)(2,1)S(1)} %get-tuple-element.9), channel_id=1, source_target_pairs={{0,8},{8,0},{16,24},{24,16},{32,40},{40,32},{48,56},{56,48},{64,72... | collective-permute-start | bytes 589832 | tf_op jit(solution)/shard_map/ppermute | solution.py:142
  5.2 8.0 %collective-permute-start.1 = (bf16[3,256,128]{2,1,0:T(8,128)(2,1)S(1)}, bf16[3,256,128]{2,1,0:T(8,128)(2,1)S(1)}, u32[]{:S(2)}, u32[]{:S(2)}) collective-permute-start(bf16[3,256,128]{2,1,0:T(8,128)(2,1)S(1)} %get-tuple-element.10), channel_id=1, source_target_pairs={{0,16},{8,24},{16,0},{24,8},{32,48},{40,56},{48,32},{56,40},{64,80... | collective-permute-start | bytes 589832 | tf_op jit(solution)/shard_map/ppermute | solution.py:142
  6.2 11.3 %collective-permute-start.2 = (bf16[3,256,128]{2,1,0:T(8,128)(2,1)S(1)}, bf16[3,256,128]{2,1,0:T(8,128)(2,1)S(1)}, u32[]{:S(2)}, u32[]{:S(2)}) collective-permute-start(bf16[3,256,128]{2,1,0:T(8,128)(2,1)S(1)} %get-tuple-element.8), channel_id=1, source_target_pairs={{0,24},{8,16},{16,8},{24,0},{32,56},{40,48},{48,40},{56,32},{64,88... | collective-permute-start | bytes 589832 | tf_op jit(solution)/shard_map/ppermute | solution.py:142
  8.5 9.3 %copy-start = (bf16[512,256]{1,0:T(8,128)(2,1)S(1)}, bf16[512,256]{1,0:T(8,128)(2,1)}, u32[]{:S(2)}) copy-start(bf16[512,256]{1,0:T(8,128)(2,1)} %constant.41.clone.fh) | copy-start | bytes 786436
  8.5 9.3 %copy-start.1 = (bf16[512,256]{1,0:T(8,128)(2,1)S(1)}, bf16[512,256]{1,0:T(8,128)(2,1)}, u32[]{:S(2)}) copy-start(bf16[512,256]{1,0:T(8,128)(2,1)} %constant.42.clone.fl) | copy-start | bytes 786436
  8.5 9.3 %copy-start.2 = (bf16[256,512]{1,0:T(8,128)(2,1)S(1)}, bf16[256,512]{1,0:T(8,128)(2,1)}, u32[]{:S(2)}) copy-start(bf16[256,512]{1,0:T(8,128)(2,1)} %constant.43.clone.ih) | copy-start | bytes 786436
  9.5 8.2 %collective-permute-start.3 = (bf16[3,256,128]{2,1,0:T(8,128)(2,1)S(1)}, bf16[3,256,128]{2,1,0:T(8,128)(2,1)S(1)}, u32[]{:S(2)}, u32[]{:S(2)}) collective-permute-start(bf16[3,256,128]{2,1,0:T(8,128)(2,1)S(1)} %get-tuple-element.6), channel_id=1, source_target_pairs={{16,48},{24,56},{32,0},{40,8},{48,80},{56,88},{64,32},{72,40},{80,... | collective-permute-start | bytes 589832 | tf_op jit(solution)/shard_map/ppermute | solution.py:147

commit v2 on v1

v2 whole, which is shorter than its diff:
```python
import jax
import jax.numpy as jnp
import ml_dtypes
import numpy as np
from jax import lax
from jax.experimental import pallas as pl
from jax.experimental.pallas import tpu as pltpu
from jax.sharding import PartitionSpec as P

LAGS = 256
FRAMES = 256
SIZE = 512
LANES = 128
GROUP = 4


def two_parts(table):
    high = table.astype(ml_dtypes.bfloat16)
    low = (table - high.astype(np.float64)).astype(ml_dtypes.bfloat16)
    return high, low


def tables():
    f = np.concatenate([np.arange(0, SIZE // 2, 2), np.arange(1, SIZE // 2, 2)])
    angle = 2.0 * np.pi * (f + 0.5) / SIZE
    ahead = angle[:, None] * np.arange(FRAMES)[None, :]
    forward = np.concatenate([np.cos(ahead), -np.sin(ahead)], 0)
    back = angle[None, :] * np.arange(LAGS)[:, None]
    inverse = np.concatenate([np.cos(back), -np.sin(back)], 1) * (2.0 / SIZE)
    return two_parts(forward), two_parts(inverse)


def dot(a, b):
    return jnp.dot(a, b, preferred_element_type=jnp.float32)


def params(mib):
    return pltpu.CompilerParams(vmem_limit_bytes=mib * 1024 * 1024)


def fold(t):
    return t[:, :LANES] + t[:, LANES : 2 * LANES] + t[:, 2 * LANES :]


def transform(raw, into, slot, block, valid, fh, fl):
    frame = lax.broadcasted_iota(jnp.int32, (FRAMES, LANES), 0) + block * FRAMES
    keep = frame < valid
    part = [
        jnp.where(keep, raw[k].astype(jnp.float32), 0.0).astype(jnp.bfloat16)
        for k in range(3)
    ]
    clean = jnp.concatenate(part, axis=1)
    into[slot] = dot(fh[...], clean) + dot(fl[...], clean)


def products(power, before, selves, pairs, rows=8):
    half = SIZE // 2
    for parity in range(2):

        def step(r, carry):
            at = pl.multiple_of(parity * (half // 2) + r * rows, rows)
            read = lambda f, lo: f(pl.ds(lo + at, rows))
            both = {k: (read(f, 0), read(f, half)) for k, f in selves.items()}
            same = sum(x * x + y * y for k, (x, y) in both.items() if k[0] == "s")
            met = [(both[a], both[b]) for a, b in pairs]
            cr = sum(x[0] * y[1] - x[1] * y[0] for x, y in met)
            ci = sum(x[0] * y[0] + x[1] * y[1] for x, y in met)
            pr = fold(same + cr if parity == 0 else same - cr)
            pi = fold(-ci if parity == 0 else ci)
            if before is not None:
                pr = pr + before[pl.ds(at, rows), :]
                pi = pi + before[pl.ds(half + at, rows), :]
            power[pl.ds(at, rows), :] = pr
            power[pl.ds(half + at, rows), :] = pi
            return carry

        lax.fori_loop(0, half // 2 // rows, step, 0)


def position():
    tm = lax.axis_index("tm")
    z, q = tm // GROUP, tm % GROUP
    return z * GROUP, q // 2, q % 2


def rows_of(ref, slot):
    return lambda at: ref[slot, at, :]


def lanes_of(piece):
    return pl.ds(pl.multiple_of(piece * LANES, LANES), LANES)


def pieces_kernel(velocities, own, across, corner, core, sems):
    q = lax.axis_index("tm") % GROUP
    copies = [
        pltpu.make_async_copy(velocities.at[:, :, lanes_of(q ^ k)], out, sems.at[k])
        for k, out in ((2, across), (3, corner), (1, core), (0, own))
    ]
    for copy in copies:
        copy.start()
    for copy in copies:
        copy.wait()


def edge_kernel(own, core, out):
    q = lax.axis_index("tm") % GROUP
    mine = (q == 0) | (q == 3)

    @pl.when(mine)
    def _():
        pltpu.sync_copy(own, out)

    @pl.when(jnp.logical_not(mine))
    def _():
        pltpu.sync_copy(core, out)


def early_kernel(valid_ref, own, core, fh, fl, spec, power):
    base, pair, c = position()
    valid = valid_ref[0]
    first = base + 2 * pair
    transform(core, spec, 1 - c, first + 1 - c, valid, fh, fl)
    transform(own, spec, c, first + c, valid, fh, fl)
    blocks = {"s0": rows_of(spec, 0), "s1": rows_of(spec, 1)}
    products(power, None, blocks, [("s0", "s1")])


def late_kernel(valid_ref, across, corner, near, early, before, fh, fl, ih, il, out, spec, power):
    base, pair, c = position()
    valid = valid_ref[0]
    first = base + 2 * (1 - pair)
    beside = jnp.where(pair == 0, base + GROUP, base - 1)
    transform(near, spec, 2, beside, valid, fh, fl)
    transform(across, spec, c, first + c, valid, fh, fl)
    transform(corner, spec, 1 - c, first + 1 - c, valid, fh, fl)
    blocks = {
        "s0": rows_of(spec, 0),
        "s1": rows_of(spec, 1),
        "n": rows_of(spec, 2),
        "e": rows_of(early, 1 - pair),
    }

    @pl.when(pair == 0)
    def _():
        products(power, before, blocks, [("e", "s0"), ("s0", "s1"), ("s1", "n")])

    @pl.when(pair == 1)
    def _():
        products(power, before, blocks, [("n", "s0"), ("s0", "s1"), ("s1", "e")])

    p = power[...]
    ph = p.astype(jnp.bfloat16)
    rest = (p - ph.astype(jnp.float32)).astype(jnp.bfloat16)
    out[...] = dot(ih[...], ph) + (dot(il[...], ph) + dot(ih[...], rest))


def finish_kernel(valid_ref, mask_ref, parts, corr, sums):
    tm = lax.axis_index("tm")
    per = corr.shape[0]
    lag = tm * per + lax.broadcasted_iota(jnp.int32, (per, LANES), 0)
    anchors = (valid_ref[0] - lag).astype(jnp.float32)
    total = jnp.zeros((per, LANES), jnp.float32)
    count = jnp.zeros((1, LANES), jnp.float32)
    for q in range(GROUP):
        lanes = slice(q * LANES, (q + 1) * LANES)
        lag_sum = parts[q]
        for z in range(1, parts.shape[0] // GROUP):
            lag_sum = lag_sum + parts[z * GROUP + q]
        weight = mask_ref[:, lanes].astype(jnp.float32)
        value = weight * lag_sum / anchors
        corr[:, lanes] = value
        total = total + value
        count = count + weight
    row = jnp.sum(total, axis=1, keepdims=True)
    real = jnp.sum(count, axis=1, keepdims=True)
    lane = lax.broadcasted_iota(jnp.int32, (per, LANES), 1)
    spread = jnp.where(lane == lax.broadcasted_iota(jnp.int32, (per, LANES), 0), row, 0.0)
    line = jnp.sum(spread, axis=0, keepdims=True)
    line = jnp.where(lane[:1] < LANES // 2, line, real)
    sums[...] = jnp.broadcast_to(line[None], sums.shape)


def average_kernel(sums, out):
    line = jnp.sum(sums[...], axis=0)
    lane = lax.broadcasted_iota(jnp.int32, line.shape, 1)
    real = jnp.max(jnp.where(lane == LANES - 1, line, 0.0), axis=1, keepdims=True)
    out[...] = (line / jnp.maximum(real, 1.0))[0, : out.shape[0]]


def body(velocities, atom_mask, valid_frames):
    count = lax.axis_size("tm")
    comps = lax.axis_size("comp")
    atoms = atom_mask.shape[0]
    per = LAGS // count
    by_axis = velocities.transpose(1, 0, 2)
    anywhere = pl.BlockSpec(memory_space=pl.ANY)
    vmem = pl.BlockSpec(memory_space=pltpu.VMEM)
    smem = pl.BlockSpec(memory_space=pltpu.SMEM)
    block = jax.ShapeDtypeStruct((3, FRAMES, LANES), velocities.dtype)
    f32 = lambda *shape: jax.ShapeDtypeStruct(shape, jnp.float32)
    cost = lambda n: pl.CostEstimate(flops=0, bytes_accessed=n, transcendentals=0)

    own, to_across, to_corner, to_core = pl.pallas_call(
        pieces_kernel,
        out_shape=(block,) * 4,
        in_specs=[anywhere],
        out_specs=(anywhere,) * 4,
        scratch_shapes=[pltpu.SemaphoreType.DMA((GROUP,))],
        compiler_params=params(1),
        name="pieces",
    )(by_axis)

    def swapped(k, piece):
        return lax.ppermute(piece, "tm", [(s, s ^ k) for s in range(count)])

    across, corner, core = swapped(2, to_across), swapped(3, to_corner), swapped(1, to_core)
    edge = pl.pallas_call(
        edge_kernel,
        out_shape=block,
        in_specs=[anywhere] * 2,
        out_specs=anywhere,
        compiler_params=params(1),
        cost_estimate=cost(2 * 3 * FRAMES * LANES * 2),
        name="edge",
    )(own, core)
    hops = [(s, s - GROUP if s % GROUP < 2 else s + GROUP) for s in range(count)]
    near = lax.ppermute(edge, "tm", [(s, d) for s, d in hops if 0 <= d < count])

    (fh, fl), (ih, il) = tables()
    early, before = pl.pallas_call(
        early_kernel,
        out_shape=(f32(2, SIZE, 3 * LANES), f32(SIZE, LANES)),
        in_specs=[smem] + [vmem] * 4,
        out_specs=(vmem, vmem),
        compiler_params=params(16),
        cost_estimate=cost(8_000_000),
        name="early_blocks",
    )(valid_frames, own, core, fh, fl)
    lag_sums = pl.pallas_call(
        late_kernel,
        out_shape=f32(LAGS, LANES),
        in_specs=[smem] + [vmem] * 9,
        out_specs=vmem,
        scratch_shapes=[
            pltpu.VMEM((3, SIZE, 3 * LANES), jnp.float32),
            pltpu.VMEM((SIZE, LANES), jnp.float32),
        ],
        compiler_params=params(16),
        name="lag_sums",
    )(valid_frames, across, corner, near, early, before, fh, fl, ih, il)

    parts = lax.all_to_all(
        lag_sums.reshape(count, per, LANES), "tm", 0, 0, tiled=True
    )
    correlation, sums = pl.pallas_call(
        finish_kernel,
        out_shape=(f32(per, atoms), f32(comps, 1, LANES)),
        in_specs=[smem, vmem, vmem],
        out_specs=(vmem, vmem),
        compiler_params=params(2),
        name="finish",
    )(valid_frames, atom_mask.reshape(1, atoms), parts)
    everyone = lax.all_to_all(sums, "comp", 0, 0, tiled=True)
    average = pl.pallas_call(
        average_kernel,
        out_shape=f32(per),
        in_specs=[vmem],
        out_specs=vmem,
        compiler_params=params(1),
        name="average",
    )(everyone)
    return correlation, average


def solution(mesh):
    return jax.shard_map(
        body,
        mesh=mesh,
        in_specs=(P("tm", None, "comp"), P("comp"), P()),
        out_specs=(P("tm", "comp"), P("tm")),
        check_vma=False,
    )
```

time: 54.7 us -> 51.7 us (0.945)
  other arithmetic: 1.78 us -> 0 us
  waiting for transfers between devices: 6.3 us -> 4.81 us
  blocking collectives: 31.5 us -> 30.4 us
  local copies, waits for them, and re-layouts: 1.23 us -> 2.13 us
    unnamed x8 -> x12, local copies, waits for them, and re-layouts: 0.02 us -> 2.13 us
    ppermute x3, waiting for transfers between devices: 6.1 us -> 4.8 us  [swapped(): return lax.ppermute(piece, 'tm', [(s, s ^ k) for s in range(count)])]
    dynamic_slice x1 -> x0, local copies, waits for them, and re-layouts: 1.22 us -> none  [piece(): lax.dynamic_slice(by_axis, (0, 0, (q ^ k) * LANES), (3, FRAMES, LANES))]
    select_n x1 -> x0, other arithmetic: 1.07 us -> none  [body(): edge = jnp.where((q == 0) | (q == 3), own, core)]
    all_to_all x1, blocking collectives: 22.2 us -> 21.4 us  [body(): lax.all_to_all(lag_sums.reshape(count, per, LANES), 'tm', 0, 0, tiled=True)]
    div x1 -> x0, other arithmetic: 0.7 us -> none  [body(): average = everyone[:, 0] / jnp.maximum(everyone[:, LANES // 2], 1.0)]
    pallas_call x2 -> x6, Pallas kernels: 4.4 us -> 4.88 us  [the longest x1 2.07 us: body(): pl.pallas_call(late_kernel, out_shape=f32(LAGS, LANES), in_specs=[smem] +...]
  transfers between devices with their start and end apart: 4 -> 4, of which waited for: 3 -> 2; matrix products, arithmetic and copies ran while one was open for 2% -> 0% of each run, Pallas kernels for 0% -> 3%
where the time goes in v2:
time: 51.7 us; the launch traced here: 51.5 us
  blocking collectives  30.4 us (59%)
  starting transfers between devices  7.85 us (15%)
  Pallas kernels  4.88 us (9%)
  waiting for transfers between devices  4.81 us (9%)
  local copies, waits for them, and re-layouts  2.13 us (4%)
  between operations  1.36 us (3%)
    all_to_all x1, blocking collectives, body(): lax.all_to_all(lag_sums.reshape(count, per, LANES), 'tm', 0, 0, tiled=True)  21.4 us
    all_to_all x1, blocking collectives, body(): everyone = lax.all_to_all(sums, 'comp', 0, 0, tiled=True)  9.01 us
    ppermute x3, starting transfers between devices, swapped(): return lax.ppermute(piece, 'tm', [(s, s ^ k) for s in range(count)])  6.56 us
    ppermute x3, waiting for transfers between devices, swapped(): return lax.ppermute(piece, 'tm', [(s, s ^ k) for s in range(count)])  4.8 us
    unnamed x12, local copies, waits for them, and re-layouts  2.13 us
    pallas_call x1, Pallas kernels, body(): pl.pallas_call(late_kernel, out_shape=f32(LAGS, LANES), in_specs=[smem] +...  2.07 us
    ppermute x1, starting transfers between devices, body(): near = lax.ppermute(edge, 'tm', [(s, d) for s, d in hops if 0 <= d < count])  1.29 us
    pallas_call x1, Pallas kernels, body(): pl.pallas_call(early_kernel, out_shape=(f32(2, SIZE, 3 * LANES), f32(SIZE...  1.16 us
  transfers between devices with their start and end apart: 4, of which 2 were waited for; matrix products, arithmetic and copies ran while one was open for 0% of the time, Pallas kernels for 3%

profile of v2, /device:TPU:1, one launch (start us, length us, event | category | flops | bytes accessed | tf_op | source)
XLA Modules:
  0.0 51.5 jit_solution(4270157335604160453)
XLA Ops:
  0.6 0.0 copy-start
  0.6 0.0 copy-start.2
  0.7 1.2 %copy-done.2 = bf16[256,3,512]{2,0,1:T(8,128)(2,1)S(1)} copy-done((bf16[256,3,512]{2,0,1:T(8,128)(2,1)S(1)}, bf16[256,3,512]{2,0,1:T(8,128)(2,1)}, u32[]{:S(2)}) %copy-start.2) | copy-done | bytes 786456
  1.8 0.2 pieces.1
  2.0 3.3 %collective-permute-start.2 = (bf16[3,256,128]{2,1,0:T(8,128)(2,1)S(1)}, bf16[3,256,128]{2,1,0:T(8,128)(2,1)S(1)}, u32[]{:S(2)}, u32[]{:S(2)}) collective-permute-start(bf16[3,256,128]{2,1,0:T(8,128)(2,1)S(1)} %get-tuple-element.13), channel_id=1, source_target_pairs={{0,8},{8,0},{16,24},{24,16},{32,40},{40,32},{48,56},{56,48},{64,72... | collective-permute-start | bytes 589832 | tf_op jit(solution)/shard_map/ppermute | solution.py:215
  5.3 1.0 %collective-permute-start = (bf16[3,256,128]{2,1,0:T(8,128)(2,1)S(1)}, bf16[3,256,128]{2,1,0:T(8,128)(2,1)S(1)}, u32[]{:S(2)}, u32[]{:S(2)}) collective-permute-start(bf16[3,256,128]{2,1,0:T(8,128)(2,1)S(1)} %get-tuple-element.10), channel_id=1, source_target_pairs={{0,16},{8,24},{16,0},{24,8},{32,48},{40,56},{48,32},{56,40},{64,80... | collective-permute-start | bytes 589832 | tf_op jit(solution)/shard_map/ppermute | solution.py:215
  6.4 2.2 %collective-permute-start.1 = (bf16[3,256,128]{2,1,0:T(8,128)(2,1)S(1)}, bf16[3,256,128]{2,1,0:T(8,128)(2,1)S(1)}, u32[]{:S(2)}, u32[]{:S(2)}) collective-permute-start(bf16[3,256,128]{2,1,0:T(8,128)(2,1)S(1)} %get-tuple-element.11), channel_id=1, source_target_pairs={{0,24},{8,16},{16,8},{24,0},{32,56},{40,48},{48,40},{56,32},{64,88... | collective-permute-start | bytes 589832 | tf_op jit(solution)/shard_map/ppermute | solution.py:215
  8.6 0.0 collective-permute-done.2.core
  8.6 0.2 edge.1
  8.8 1.3 %collective-permute-start.3 = (bf16[3,256,128]{2,1,0:T(8,128)(2,1)S(1)}, bf16[3,256,128]{2,1,0:T(8,128)(2,1)S(1)}, u32[]{:S(2)}, u32[]{:S(2)}) collective-permute-start(bf16[3,256,128]{2,1,0:T(8,128)(2,1)S(1)} %edge.1), channel_id=1, source_target_pairs={{16,48},{24,56},{32,0},{40,8},{48,80},{56,88},{64,32},{72,40},{80,... | collective-permute-start | bytes 589832 | tf_op jit(solution)/shard_map/ppermute | solution.py:228
  10.8 0.0 copy-done
  10.8 0.0 copy-start.1
  10.8 0.9 %copy-done.1 = bf16[512,256]{1,0:T(8,128)(2,1)S(1)} copy-done((bf16[512,256]{1,0:T(8,128)(2,1)S(1)}, bf16[512,256]{1,0:T(8,128)(2,1)}, u32[]{:S(2)}) %copy-start.1) | copy-done | bytes 262168
  11.7 1.2 %early_blocks.1 = (f32[2,512,384]{2,1,0:T(8,128)S(1)}, f32[512,128]{1,0:T(8,128)S(1)}) custom-call(s32[1]{0:T(128)S(6)} %copy.9.valid_ref, bf16[3,256,128]{2,1,0:T(8,128)(2,1)S(1)} %get-tuple-element.12.own, bf16[3,256,128]{2,1,0:T(8,128)(2,1)S(1)} %collective-permute-done.2.core, bf16[512,256]{1,0:T(8,128)(2,1)S(1)} %copy-done.1, bf16[512,256]{1,0:T(8,128)(2,1)S(1)} %copy-done), custom_call_target="tpu_custom_call" | custom-call | bytes 8000000 | tf_op jit(solution)/shard_map/early_blocks/pallas_call | solution.py:231
  12.9 0.4 collective-permute-done.across
  13.3 4.4 %collective-permute-done.1.corner = bf16[3,256,128]{2,1,0:T(8,128)(2,1)S(1)} collective-permute-done((bf16[3,256,128]{2,1,0:T(8,128)(2,1)S(1)}, bf16[3,256,128]{2,1,0:T(8,128)(2,1)S(1)}, u32[]{:S(2)}, u32[]{:S(2)}) %collective-permute-start.1) | collective-permute-done | bytes 196640 | tf_op jit(solution)/shard_map/ppermute | solution.py:215
  17.7 0.0 collective-permute-done.3.near
  17.7 0.0 copy-done.3
  17.7 0.0 copy-start.5
  17.7 2.1 %lag_sums.1 = f32[256,128]{1,0:T(8,128)S(1)} custom-call(s32[1]{0:T(128)S(6)} %copy.9.valid_ref, bf16[3,256,128]{2,1,0:T(8,128)(2,1)S(1)} %collective-permute-done.across, bf16[3,256,128]{2,1,0:T(8,128)(2,1)S(1)} %collective-permute-done.1.corner, bf16[3,256,128]{2,1,0:T(8,128)(2,1)S(1)} %collective-permute-done.3.near, ...), custom_call_target="tpu_custom_call" | custom-call | tf_op jit(solution)/shard_map/lag_sums/pallas_call | solution.py:240
  19.8 21.4 %all_to_all.10.parts = f32[32,8,128]{2,1,0:T(8,128)S(1)} all-to-all(f32[32,8,128]{2,1,0:T(8,128)S(1)} %bitcast.4), channel_id=1, replica_groups=mesh['tm'=32,'comp'=8] {'tm'}, dimensions={0} | all-to-all | bytes 262144 | tf_op jit(solution)/shard_map/all_to_all | solution.py:253
  41.2 0.6 %finish.1 = (f32[8,512]{1,0:T(8,128)}, f32[8,1,128]{2,1,0:T(1,128)S(1)}) custom-call(s32[1]{0:T(128)S(6)} %copy.9.valid_ref, s32[1,512]{1,0:T(1,128)S(1)} %bitcast.5, f32[32,8,128]{2,1,0:T(8,128)S(1)} %all_to_all.10.parts), custom_call_target="tpu_custom_call" | custom-call | tf_op jit(solution)/shard_map/finish/pallas_call | solution.py:256
  41.9 9.0 %all_to_all.11.sums = f32[8,1,128]{2,1,0:T(1,128)S(1)} all-to-all(f32[8,1,128]{2,1,0:T(1,128)S(1)} %get-tuple-element.17), channel_id=1, replica_groups=mesh['tm'=32,'comp'=8] {'comp'}, dimensions={0} | all-to-all | bytes 8192 | tf_op jit(solution)/shard_map/all_to_all | solution.py:264
  50.9 0.6 %average.1 = f32[8]{0:T(128)} custom-call(f32[8,1,128]{2,1,0:T(1,128)S(1)} %all_to_all.11.sums), custom_call_target="tpu_custom_call" | custom-call | tf_op jit(solution)/shard_map/average/pallas_call | solution.py:265
  (4 shorter events, 0.0 us)
Async XLA Ops:
  0.6 10.1 %copy-start = (bf16[512,256]{1,0:T(8,128)(2,1)S(1)}, bf16[512,256]{1,0:T(8,128)(2,1)}, u32[]{:S(2)}) copy-start(bf16[512,256]{1,0:T(8,128)(2,1)} %constant.9.clone.fl) | copy-start | bytes 786436
  0.6 1.2 %copy-start.2 = (bf16[256,3,512]{2,0,1:T(8,128)(2,1)S(1)}, bf16[256,3,512]{2,0,1:T(8,128)(2,1)}, u32[]{:S(2)}) copy-start(bf16[256,3,512]{2,0,1:T(8,128)(2,1)} %param.7) | copy-start | bytes 2359300
  1.8 15.9 %copy-start.3 = (bf16[256,512]{1,0:T(8,128)(2,1)S(1)}, bf16[256,512]{1,0:T(8,128)(2,1)}, u32[]{:S(2)}) copy-start(bf16[256,512]{1,0:T(8,128)(2,1)} %constant.11.clone.il) | copy-start | bytes 786436
  1.8 15.9 %copy-start.4 = (bf16[256,512]{1,0:T(8,128)(2,1)S(1)}, bf16[256,512]{1,0:T(8,128)(2,1)}, u32[]{:S(2)}) copy-start(bf16[256,512]{1,0:T(8,128)(2,1)} %constant.10.clone.ih) | copy-start | bytes 786436
  2.0 6.6 %collective-permute-start.2 = (bf16[3,256,128]{2,1,0:T(8,128)(2,1)S(1)}, bf16[3,256,128]{2,1,0:T(8,128)(2,1)S(1)}, u32[]{:S(2)}, u32[]{:S(2)}) collective-permute-start(bf16[3,256,128]{2,1,0:T(8,128)(2,1)S(1)} %get-tuple-element.13), channel_id=1, source_target_pairs={{0,8},{8,0},{16,24},{24,16},{32,40},{40,32},{48,56},{56,48},{64,72... | collective-permute-start | bytes 589832 | tf_op jit(solution)/shard_map/ppermute | solution.py:215
  5.3 8.0 %collective-permute-start = (bf16[3,256,128]{2,1,0:T(8,128)(2,1)S(1)}, bf16[3,256,128]{2,1,0:T(8,128)(2,1)S(1)}, u32[]{:S(2)}, u32[]{:S(2)}) collective-permute-start(bf16[3,256,128]{2,1,0:T(8,128)(2,1)S(1)} %get-tuple-element.10), channel_id=1, source_target_pairs={{0,16},{8,24},{16,0},{24,8},{32,48},{40,56},{48,32},{56,40},{64,80... | collective-permute-start | bytes 589832 | tf_op jit(solution)/shard_map/ppermute | solution.py:215
  6.4 11.3 %collective-permute-start.1 = (bf16[3,256,128]{2,1,0:T(8,128)(2,1)S(1)}, bf16[3,256,128]{2,1,0:T(8,128)(2,1)S(1)}, u32[]{:S(2)}, u32[]{:S(2)}) collective-permute-start(bf16[3,256,128]{2,1,0:T(8,128)(2,1)S(1)} %get-tuple-element.11), channel_id=1, source_target_pairs={{0,24},{8,16},{16,8},{24,0},{32,56},{40,48},{48,40},{56,32},{64,88... | collective-permute-start | bytes 589832 | tf_op jit(solution)/shard_map/ppermute | solution.py:215
  8.8 8.9 %collective-permute-start.3 = (bf16[3,256,128]{2,1,0:T(8,128)(2,1)S(1)}, bf16[3,256,128]{2,1,0:T(8,128)(2,1)S(1)}, u32[]{:S(2)}, u32[]{:S(2)}) collective-permute-start(bf16[3,256,128]{2,1,0:T(8,128)(2,1)S(1)} %edge.1), channel_id=1, source_target_pairs={{16,48},{24,56},{32,0},{40,8},{48,80},{56,88},{64,32},{72,40},{80,... | collective-permute-start | bytes 589832 | tf_op jit(solution)/shard_map/ppermute | solution.py:228
  10.8 1.0 %copy-start.1 = (bf16[512,256]{1,0:T(8,128)(2,1)S(1)}, bf16[512,256]{1,0:T(8,128)(2,1)}, u32[]{:S(2)}) copy-start(bf16[512,256]{1,0:T(8,128)(2,1)} %constant.8.clone.fh) | copy-start | bytes 786436
  17.7 23.5 %copy-start.5 = (s32[512]{0:T(512)S(1)}, s32[512]{0:T(512)}, u32[]{:S(2)}) copy-start(s32[512]{0:T(512)} %param.8) | copy-start | bytes 6148

commit v3 on v2

--- a/solution.py
+++ b/solution.py
@@ -1,3 +1,5 @@
+import functools
+
 import jax
 import jax.numpy as jnp
 import ml_dtypes
@@ -53,20 +55,21 @@
     into[slot] = dot(fh[...], clean) + dot(fl[...], clean)
 
 
-def products(power, before, selves, pairs, rows=8):
+def products(power, before, blocks, alone, pairs, rows=8):
     half = SIZE // 2
     for parity in range(2):
 
         def step(r, carry):
             at = pl.multiple_of(parity * (half // 2) + r * rows, rows)
             read = lambda f, lo: f(pl.ds(lo + at, rows))
-            both = {k: (read(f, 0), read(f, half)) for k, f in selves.items()}
-            same = sum(x * x + y * y for k, (x, y) in both.items() if k[0] == "s")
+            both = [(read(f, 0), read(f, half)) for f in blocks]
+            same = sum(both[k][0] * both[k][0] + both[k][1] * both[k][1] for k in alone)
             met = [(both[a], both[b]) for a, b in pairs]
-            cr = sum(x[0] * y[1] - x[1] * y[0] for x, y in met)
-            ci = sum(x[0] * y[0] + x[1] * y[1] for x, y in met)
-            pr = fold(same + cr if parity == 0 else same - cr)
-            pi = fold(-ci if parity == 0 else ci)
+            pr, pi = fold(same), 0.0
+            if met:
+                cr = fold(sum(x[0] * y[1] - x[1] * y[0] for x, y in met))
+                ci = fold(sum(x[0] * y[0] + x[1] * y[1] for x, y in met))
+                pr, pi = (pr + cr, -ci) if parity == 0 else (pr - cr, ci)
             if before is not None:
                 pr = pr + before[pl.ds(at, rows), :]
                 pi = pi + before[pl.ds(half + at, rows), :]
@@ -91,11 +94,12 @@
     return pl.ds(pl.multiple_of(piece * LANES, LANES), LANES)
 
 
-def pieces_kernel(velocities, own, across, corner, core, sems):
+def pieces_kernel(which, velocities, *rest):
+    *outs, sems = rest
     q = lax.axis_index("tm") % GROUP
     copies = [
-        pltpu.make_async_copy(velocities.at[:, :, lanes_of(q ^ k)], out, sems.at[k])
-        for k, out in ((2, across), (3, corner), (1, core), (0, own))
+        pltpu.make_async_copy(velocities.at[:, :, lanes_of(q ^ k)], out, sems.at[n])
+        for n, (k, out) in enumerate(zip(which, outs))
     ]
     for copy in copies:
         copy.start()
@@ -122,54 +126,70 @@
     first = base + 2 * pair
     transform(core, spec, 1 - c, first + 1 - c, valid, fh, fl)
     transform(own, spec, c, first + c, valid, fh, fl)
-    blocks = {"s0": rows_of(spec, 0), "s1": rows_of(spec, 1)}
-    products(power, None, blocks, [("s0", "s1")])
-
-
-def late_kernel(valid_ref, across, corner, near, early, before, fh, fl, ih, il, out, spec, power):
+    products(power, None, [rows_of(spec, 0), rows_of(spec, 1)], [0, 1], [(0, 1)])
+
+
+def in_order(case, early, near, across, corner):
+    ends = [rows_of(early, 1 - case // 2), near]
+    late = [across, corner]
+    if case // 2:
+        ends.reverse()
+    if case % 2:
+        late.reverse()
+    return [ends[0], *late, ends[1]]
+
+
+def middle_kernel(valid_ref, near, across, early, before, fh, fl, spec, power):
     base, pair, c = position()
     valid = valid_ref[0]
-    first = base + 2 * (1 - pair)
     beside = jnp.where(pair == 0, base + GROUP, base - 1)
-    transform(near, spec, 2, beside, valid, fh, fl)
-    transform(across, spec, c, first + c, valid, fh, fl)
-    transform(corner, spec, 1 - c, first + 1 - c, valid, fh, fl)
-    blocks = {
-        "s0": rows_of(spec, 0),
-        "s1": rows_of(spec, 1),
-        "n": rows_of(spec, 2),
-        "e": rows_of(early, 1 - pair),
-    }
-
-    @pl.when(pair == 0)
-    def _():
-        products(power, before, blocks, [("e", "s0"), ("s0", "s1"), ("s1", "n")])
-
-    @pl.when(pair == 1)
-    def _():
-        products(power, before, blocks, [("n", "s0"), ("s0", "s1"), ("s1", "e")])
+    transform(near, spec, 1, beside, valid, fh, fl)
+    transform(across, spec, 0, base + 2 * (1 - pair) + c, valid, fh, fl)
+    for case in range(GROUP):
+        line = in_order(case, early, rows_of(spec, 1), rows_of(spec, 0), None)
+        line = line[2:] if case % 2 else line[:2]
+
+        @pl.when(2 * pair + c == case)
+        def _(line=line, case=case):
+            products(power, before, line, [1 - case % 2], [(0, 1)])
+
+
+def late_kernel(valid_ref, corner, early, middle, before, fh, fl, ih, il, out, spec, power):
+    base, pair, c = position()
+    block = base + 2 * (1 - pair) + 1 - c
+    transform(corner, spec, 0, block, valid_ref[0], fh, fl)
+    for case in range(GROUP):
+        line = in_order(case, early, rows_of(middle, 1), rows_of(middle, 0), rows_of(spec, 0))
+        line = line[:3] if case % 2 else line[1:]
+
+        @pl.when(2 * pair + c == case)
+        def _(line=line):
+            products(power, before, line, [1], [(0, 1), (1, 2)])
 
     p = power[...]
     ph = p.astype(jnp.bfloat16)
     rest = (p - ph.astype(jnp.float32)).astype(jnp.bfloat16)
-    out[...] = dot(ih[...], ph) + (dot(il[...], ph) + dot(ih[...], rest))
-
-
-def finish_kernel(valid_ref, mask_ref, parts, corr, sums):
-    tm = lax.axis_index("tm")
-    per = corr.shape[0]
-    lag = tm * per + lax.broadcasted_iota(jnp.int32, (per, LANES), 0)
+    both = dot(ih[...], jnp.concatenate([ph, rest], axis=1))
+    out[...] = both[:, :LANES] + (dot(il[...], ph) + both[:, LANES:])
+
+
+def correlations(valid_ref, mask_ref, parts):
+    per = parts.shape[1]
+    lag = lax.axis_index("tm") * per + lax.broadcasted_iota(jnp.int32, (per, LANES), 0)
     anchors = (valid_ref[0] - lag).astype(jnp.float32)
-    total = jnp.zeros((per, LANES), jnp.float32)
-    count = jnp.zeros((1, LANES), jnp.float32)
     for q in range(GROUP):
-        lanes = slice(q * LANES, (q + 1) * LANES)
         lag_sum = parts[q]
         for z in range(1, parts.shape[0] // GROUP):
             lag_sum = lag_sum + parts[z * GROUP + q]
-        weight = mask_ref[:, lanes].astype(jnp.float32)
-        value = weight * lag_sum / anchors
-        corr[:, lanes] = value
+        weight = mask_ref[:, q * LANES : (q + 1) * LANES].astype(jnp.float32)
+        yield q, weight, weight * lag_sum / anchors
+
+
+def sums_kernel(valid_ref, mask_ref, parts, sums):
+    per = parts.shape[1]
+    total = jnp.zeros((per, LANES), jnp.float32)
+    count = jnp.zeros((1, LANES), jnp.float32)
+    for _, weight, value in correlations(valid_ref, mask_ref, parts):
         total = total + value
         count = count + weight
     row = jnp.sum(total, axis=1, keepdims=True)
@@ -181,11 +201,13 @@
     sums[...] = jnp.broadcast_to(line[None], sums.shape)
 
 
-def average_kernel(sums, out):
-    line = jnp.sum(sums[...], axis=0)
+def finish_kernel(valid_ref, mask_ref, parts, everyone, corr, average):
+    for q, _, value in correlations(valid_ref, mask_ref, parts):
+        corr[:, q * LANES : (q + 1) * LANES] = value
+    line = jnp.sum(everyone[...], axis=0)
     lane = lax.broadcasted_iota(jnp.int32, line.shape, 1)
     real = jnp.max(jnp.where(lane == LANES - 1, line, 0.0), axis=1, keepdims=True)
-    out[...] = (line / jnp.maximum(real, 1.0))[0, : out.shape[0]]
+    average[...] = (line / jnp.maximum(real, 1.0))[0, : average.shape[0]]
 
 
 def body(velocities, atom_mask, valid_frames):
@@ -201,20 +223,21 @@
     f32 = lambda *shape: jax.ShapeDtypeStruct(shape, jnp.float32)
     cost = lambda n: pl.CostEstimate(flops=0, bytes_accessed=n, transcendentals=0)
 
-    own, to_across, to_corner, to_core = pl.pallas_call(
-        pieces_kernel,
-        out_shape=(block,) * 4,
+    order = (1, 2, 3, 0)
+    to_core, to_across, to_corner, own = pl.pallas_call(
+        functools.partial(pieces_kernel, order),
+        out_shape=(block,) * len(order),
         in_specs=[anywhere],
-        out_specs=(anywhere,) * 4,
-        scratch_shapes=[pltpu.SemaphoreType.DMA((GROUP,))],
-        compiler_params=params(1),
+        out_specs=(anywhere,) * len(order),
+        scratch_shapes=[pltpu.SemaphoreType.DMA((len(order),))],
+        compiler_params=params(53),
         name="pieces",
     )(by_axis)
 
     def swapped(k, piece):
         return lax.ppermute(piece, "tm", [(s, s ^ k) for s in range(count)])
 
-    across, corner, core = swapped(2, to_across), swapped(3, to_corner), swapped(1, to_core)
+    core, across, corner = swapped(1, to_core), swapped(2, to_across), swapped(3, to_corner)
     edge = pl.pallas_call(
         edge_kernel,
         out_shape=block,
@@ -237,39 +260,48 @@
         cost_estimate=cost(8_000_000),
         name="early_blocks",
     )(valid_frames, own, core, fh, fl)
+    middle, before = pl.pallas_call(
+        middle_kernel,
+        out_shape=(f32(2, SIZE, 3 * LANES), f32(SIZE, LANES)),
+        in_specs=[smem] + [vmem] * 6,
+        out_specs=(vmem, vmem),
+        compiler_params=params(8),
+        name="middle_block",
+    )(valid_frames, near, across, early, before, fh, fl)
     lag_sums = pl.pallas_call(
         late_kernel,
         out_shape=f32(LAGS, LANES),
-        in_specs=[smem] + [vmem] * 9,
+        in_specs=[smem] + [vmem] * 8,
         out_specs=vmem,
         scratch_shapes=[
-            pltpu.VMEM((3, SIZE, 3 * LANES), jnp.float32),
+            pltpu.VMEM((1, SIZE, 3 * LANES), jnp.float32),
             pltpu.VMEM((SIZE, LANES), jnp.float32),
         ],
         compiler_params=params(16),
         name="lag_sums",
-    )(valid_frames, across, corner, near, early, before, fh, fl, ih, il)
+    )(valid_frames, corner, early, middle, before, fh, fl, ih, il)
 
     parts = lax.all_to_all(
         lag_sums.reshape(count, per, LANES), "tm", 0, 0, tiled=True
     )
-    correlation, sums = pl.pallas_call(
+    mask = atom_mask.reshape(1, atoms)
+    sums = pl.pallas_call(
+        sums_kernel,
+        out_shape=f32(comps, 1, LANES),
+        in_specs=[smem, vmem, vmem],
+        out_specs=vmem,
+        compiler_params=params(2),
+        name="sums",
+    )(valid_frames, mask, parts)
+    everyone = lax.all_to_all(sums, "comp", 0, 0, tiled=True)
+    correlation, average = pl.pallas_call(
         finish_kernel,
-        out_shape=(f32(per, atoms), f32(comps, 1, LANES)),
-        in_specs=[smem, vmem, vmem],
+        out_shape=(f32(per, atoms), f32(per)),
+        in_specs=[smem, vmem, vmem, vmem],
         out_specs=(vmem, vmem),
         compiler_params=params(2),
         name="finish",
-    )(valid_frames, atom_mask.reshape(1, atoms), parts)
-    everyone = lax.all_to_all(sums, "comp", 0, 0, tiled=True)
-    average = pl.pallas_call(
-        average_kernel,
-        out_shape=f32(per),
-        in_specs=[vmem],
-        out_specs=vmem,
-        compiler_params=params(1),
-        name="average",
-    )(everyone)
+    )(valid_frames, mask, parts, everyone)
     return correlation, average
 
 

time: 51.7 us -> 49.9 us (0.965)
  waiting for transfers between devices: 4.81 us -> 1.93 us
  starting transfers between devices: 7.85 us -> 9.54 us
  local copies, waits for them, and re-layouts: 2.13 us -> 0.98 us
  Pallas kernels: 4.88 us -> 5.85 us
    ppermute x3, waiting for transfers between devices: 4.8 us -> 1.62 us  [swapped(): return lax.ppermute(piece, 'tm', [(s, s ^ k) for s in range(count)])]
    pallas_call x3 -> x4, Pallas kernels: 1.41 us -> 3.19 us  [the longest x1 1.32 us: body(): pl.pallas_call(functools.partial(pieces_kernel, order), out_shape=(block,...]
    ppermute x3, starting transfers between devices: 6.56 us -> 8.25 us  [swapped(): return lax.ppermute(piece, 'tm', [(s, s ^ k) for s in range(count)])]
    unnamed x12, local copies, waits for them, and re-layouts: 2.13 us -> 0.98 us
    pallas_call x1, Pallas kernels: 2.07 us -> 1.28 us  [body(): pl.pallas_call(late_kernel, out_shape=f32(LAGS, LANES), in_specs=[smem] +...]
  transfers between devices with their start and end apart: 4 -> 4, of which waited for: 2 -> 2; matrix products, arithmetic and copies ran while one was open for 0% -> 0% of each run, Pallas kernels for 3% -> 5%
where the time goes in v3:
time: 49.9 us; the launch traced here: 49.7 us
  blocking collectives  30 us (60%)
  starting transfers between devices  9.54 us (19%)
  Pallas kernels  5.85 us (12%)
  waiting for transfers between devices  1.93 us (4%)
  between operations  1.4 us (3%)
  local copies, waits for them, and re-layouts  0.98 us (2%)
    all_to_all x1, blocking collectives, body(): lax.all_to_all(lag_sums.reshape(count, per, LANES), 'tm', 0, 0, tiled=True)  20.9 us
    all_to_all x1, blocking collectives, body(): everyone = lax.all_to_all(sums, 'comp', 0, 0, tiled=True)  9.07 us
    ppermute x3, starting transfers between devices, swapped(): return lax.ppermute(piece, 'tm', [(s, s ^ k) for s in range(count)])  8.25 us
    ppermute x3, waiting for transfers between devices, swapped(): return lax.ppermute(piece, 'tm', [(s, s ^ k) for s in range(count)])  1.62 us
    pallas_call x1, Pallas kernels, body(): pl.pallas_call(functools.partial(pieces_kernel, order), out_shape=(block,...  1.32 us
    ppermute x1, starting transfers between devices, body(): near = lax.ppermute(edge, 'tm', [(s, d) for s, d in hops if 0 <= d < count])  1.29 us
    pallas_call x1, Pallas kernels, body(): pl.pallas_call(late_kernel, out_shape=f32(LAGS, LANES), in_specs=[smem] +...  1.28 us
    pallas_call x1, Pallas kernels, body(): pl.pallas_call(early_kernel, out_shape=(f32(2, SIZE, 3 * LANES), f32(SIZE...  1.16 us
  transfers between devices with their start and end apart: 4, of which 2 were waited for; matrix products, arithmetic and copies ran while one was open for 0% of the time, Pallas kernels for 5%

profile of v3, /device:TPU:1, one launch (start us, length us, event | category | flops | bytes accessed | tf_op | source)
XLA Modules:
  0.0 49.7 jit_solution(491529354708954886)
XLA Ops:
  0.6 0.0 copy-start
  0.6 1.3 %pieces.1 = (bf16[3,256,128]{2,1,0:T(8,128)(2,1)S(1)}, bf16[3,256,128]{2,1,0:T(8,128)(2,1)S(1)}, bf16[3,256,128]{2,1,0:T(8,128)(2,1)S(1)}, bf16[3,256,128]{2,1,0:T(8,128)(2,1)S(1)}) custom-call(bf16[3,256,512]{2,1,0:T(8,128)(2,1)} %bitcast.6), custom_call_target="tpu_custom_call" | custom-call | tf_op jit(solution)/shard_map/pieces/pallas_call | solution.py:227
  2.0 3.3 %collective-permute-start.1 = (bf16[3,256,128]{2,1,0:T(8,128)(2,1)S(1)}, bf16[3,256,128]{2,1,0:T(8,128)(2,1)S(1)}, u32[]{:S(2)}, u32[]{:S(2)}) collective-permute-start(bf16[3,256,128]{2,1,0:T(8,128)(2,1)S(1)} %get-tuple-element.12), channel_id=1, source_target_pairs={{0,8},{8,0},{16,24},{24,16},{32,40},{40,32},{48,56},{56,48},{64,72... | collective-permute-start | bytes 589832 | tf_op jit(solution)/shard_map/ppermute | solution.py:238
  5.3 1.0 %collective-permute-start.3 = (bf16[3,256,128]{2,1,0:T(8,128)(2,1)S(1)}, bf16[3,256,128]{2,1,0:T(8,128)(2,1)S(1)}, u32[]{:S(2)}, u32[]{:S(2)}) collective-permute-start(bf16[3,256,128]{2,1,0:T(8,128)(2,1)S(1)} %get-tuple-element.14), channel_id=1, source_target_pairs={{0,16},{8,24},{16,0},{24,8},{32,48},{40,56},{48,32},{56,40},{64,80... | collective-permute-start | bytes 589832 | tf_op jit(solution)/shard_map/ppermute | solution.py:238
  6.3 0.0 collective-permute-done.1.core
  6.4 0.2 edge.1
  6.6 1.3 %collective-permute-start.2 = (bf16[3,256,128]{2,1,0:T(8,128)(2,1)S(1)}, bf16[3,256,128]{2,1,0:T(8,128)(2,1)S(1)}, u32[]{:S(2)}, u32[]{:S(2)}) collective-permute-start(bf16[3,256,128]{2,1,0:T(8,128)(2,1)S(1)} %edge.1), channel_id=1, source_target_pairs={{16,48},{24,56},{32,0},{40,8},{48,80},{56,88},{64,32},{72,40},{80,... | collective-permute-start | bytes 589832 | tf_op jit(solution)/shard_map/ppermute | solution.py:251
  7.9 3.9 %collective-permute-start = (bf16[3,256,128]{2,1,0:T(8,128)(2,1)S(1)}, bf16[3,256,128]{2,1,0:T(8,128)(2,1)S(1)}, u32[]{:S(2)}, u32[]{:S(2)}) collective-permute-start(bf16[3,256,128]{2,1,0:T(8,128)(2,1)S(1)} %get-tuple-element.10), channel_id=1, source_target_pairs={{0,24},{8,16},{16,8},{24,0},{32,56},{40,48},{48,40},{56,32},{64,88... | collective-permute-start | bytes 589832 | tf_op jit(solution)/shard_map/ppermute | solution.py:238
  12.5 0.0 copy-start.1
  12.5 0.9 %copy-done.1 = bf16[512,256]{1,0:T(8,128)(2,1)S(1)} copy-done((bf16[512,256]{1,0:T(8,128)(2,1)S(1)}, bf16[512,256]{1,0:T(8,128)(2,1)}, u32[]{:S(2)}) %copy-start.1) | copy-done | bytes 262168
  13.4 1.2 %early_blocks.1 = (f32[2,512,384]{2,1,0:T(8,128)S(1)}, f32[512,128]{1,0:T(8,128)S(1)}) custom-call(s32[1]{0:T(128)S(6)} %copy.9.valid_ref, bf16[3,256,128]{2,1,0:T(8,128)(2,1)S(1)} %get-tuple-element.11.own, bf16[3,256,128]{2,1,0:T(8,128)(2,1)S(1)} %collective-permute-done.1.core, bf16[512,256]{1,0:T(8,128)(2,1)S(1)} %copy-done.1, bf16[512,256]{1,0:T(8,128)(2,1)S(1)} %copy-done), custom_call_target="tpu_custom_call" | custom-call | bytes 8000000 | tf_op jit(solution)/shard_map/early_blocks/pallas_call | solution.py:254
  14.6 0.0 copy-start.2
  14.6 0.0 copy-start.3
  14.6 0.0 copy-start.4
  14.6 0.0 collective-permute-done.3.across
  14.6 0.3 collective-permute-done.2.near
  14.9 1.1 %middle_block.1 = (f32[2,512,384]{2,1,0:T(8,128)S(1)}, f32[512,128]{1,0:T(8,128)S(1)}) custom-call(s32[1]{0:T(128)S(6)} %copy.9.valid_ref, bf16[3,256,128]{2,1,0:T(8,128)(2,1)S(1)} %collective-permute-done.2.near, bf16[3,256,128]{2,1,0:T(8,128)(2,1)S(1)} %collective-permute-done.3.across, f32[2,512,384]{2,1,0:T(8,128)S(1)} %get-tuple-element.13.early, ...), custom_call_target="tpu_custom_call" | custom-call | tf_op jit(solution)/shard_map/middle_block/pallas_call | solution.py:263
  16.1 1.6 %collective-permute-done.corner = bf16[3,256,128]{2,1,0:T(8,128)(2,1)S(1)} collective-permute-done((bf16[3,256,128]{2,1,0:T(8,128)(2,1)S(1)}, bf16[3,256,128]{2,1,0:T(8,128)(2,1)S(1)}, u32[]{:S(2)}, u32[]{:S(2)}) %collective-permute-start) | collective-permute-done | bytes 196640 | tf_op jit(solution)/shard_map/ppermute | solution.py:238
  17.7 0.0 copy-start.5
  17.7 1.3 %lag_sums.1 = f32[256,128]{1,0:T(8,128)S(1)} custom-call(s32[1]{0:T(128)S(6)} %copy.9.valid_ref, bf16[3,256,128]{2,1,0:T(8,128)(2,1)S(1)} %collective-permute-done.corner, f32[2,512,384]{2,1,0:T(8,128)S(1)} %get-tuple-element.13.early, f32[2,512,384]{2,1,0:T(8,128)S(1)} %get-tuple-element.16.middle, f32[512,128]{1,0:T(8,128)S(1)} %get-tuple-element.17.before, ...), custom_call_target="tpu_custom_call" | custom-call | tf_op jit(solution)/shard_map/lag_sums/pallas_call | solution.py:271
  19.0 20.9 %all_to_all.10.parts = f32[32,8,128]{2,1,0:T(8,128)S(1)} all-to-all(f32[32,8,128]{2,1,0:T(8,128)S(1)} %bitcast.3), channel_id=1, replica_groups=mesh['tm'=32,'comp'=8] {'tm'}, dimensions={0} | all-to-all | bytes 262144 | tf_op jit(solution)/shard_map/all_to_all | solution.py:284
  39.9 0.1 sums.1
  40.0 9.1 %all_to_all.11.everyone = f32[8,1,128]{2,1,0:T(1,128)S(1)} all-to-all(f32[8,1,128]{2,1,0:T(1,128)S(1)} %sums.1), channel_id=1, replica_groups=mesh['tm'=32,'comp'=8] {'comp'}, dimensions={0} | all-to-all | bytes 8192 | tf_op jit(solution)/shard_map/all_to_all | solution.py:296
  49.1 0.6 %finish.1 = (f32[8,512]{1,0:T(8,128)}, f32[8]{0:T(128)}) custom-call(s32[1]{0:T(128)S(6)} %copy.9.valid_ref, s32[1,512]{1,0:T(1,128)S(1)} %bitcast.5, f32[32,8,128]{2,1,0:T(8,128)S(1)} %all_to_all.10.parts, f32[8,1,128]{2,1,0:T(1,128)S(1)} %all_to_all.11.everyone), custom_call_target="tpu_custom_call" | custom-call | tf_op jit(solution)/shard_map/finish/pallas_call | solution.py:297
  (5 shorter events, 0.0 us)
Async XLA Ops:
  0.6 11.8 %copy-start = (bf16[512,256]{1,0:T(8,128)(2,1)S(1)}, bf16[512,256]{1,0:T(8,128)(2,1)}, u32[]{:S(2)}) copy-start(bf16[512,256]{1,0:T(8,128)(2,1)} %constant.9.clone.fl) | copy-start | bytes 786436
  2.0 4.4 %collective-permute-start.1 = (bf16[3,256,128]{2,1,0:T(8,128)(2,1)S(1)}, bf16[3,256,128]{2,1,0:T(8,128)(2,1)S(1)}, u32[]{:S(2)}, u32[]{:S(2)}) collective-permute-start(bf16[3,256,128]{2,1,0:T(8,128)(2,1)S(1)} %get-tuple-element.12), channel_id=1, source_target_pairs={{0,8},{8,0},{16,24},{24,16},{32,40},{40,32},{48,56},{56,48},{64,72... | collective-permute-start | bytes 589832 | tf_op jit(solution)/shard_map/ppermute | solution.py:238
  5.3 9.3 %collective-permute-start.3 = (bf16[3,256,128]{2,1,0:T(8,128)(2,1)S(1)}, bf16[3,256,128]{2,1,0:T(8,128)(2,1)S(1)}, u32[]{:S(2)}, u32[]{:S(2)}) collective-permute-start(bf16[3,256,128]{2,1,0:T(8,128)(2,1)S(1)} %get-tuple-element.14), channel_id=1, source_target_pairs={{0,16},{8,24},{16,0},{24,8},{32,48},{40,56},{48,32},{56,40},{64,80... | collective-permute-start | bytes 589832 | tf_op jit(solution)/shard_map/ppermute | solution.py:238
  6.6 8.3 %collective-permute-start.2 = (bf16[3,256,128]{2,1,0:T(8,128)(2,1)S(1)}, bf16[3,256,128]{2,1,0:T(8,128)(2,1)S(1)}, u32[]{:S(2)}, u32[]{:S(2)}) collective-permute-start(bf16[3,256,128]{2,1,0:T(8,128)(2,1)S(1)} %edge.1), channel_id=1, source_target_pairs={{16,48},{24,56},{32,0},{40,8},{48,80},{56,88},{64,32},{72,40},{80,... | collective-permute-start | bytes 589832 | tf_op jit(solution)/shard_map/ppermute | solution.py:251
  7.9 9.8 %collective-permute-start = (bf16[3,256,128]{2,1,0:T(8,128)(2,1)S(1)}, bf16[3,256,128]{2,1,0:T(8,128)(2,1)S(1)}, u32[]{:S(2)}, u32[]{:S(2)}) collective-permute-start(bf16[3,256,128]{2,1,0:T(8,128)(2,1)S(1)} %get-tuple-element.10), channel_id=1, source_target_pairs={{0,24},{8,16},{16,8},{24,0},{32,56},{40,48},{48,40},{56,32},{64,88... | collective-permute-start | bytes 589832 | tf_op jit(solution)/shard_map/ppermute | solution.py:238
  12.5 1.0 %copy-start.1 = (bf16[512,256]{1,0:T(8,128)(2,1)S(1)}, bf16[512,256]{1,0:T(8,128)(2,1)}, u32[]{:S(2)}) copy-start(bf16[512,256]{1,0:T(8,128)(2,1)} %constant.8.clone.fh) | copy-start | bytes 786436
  14.6 3.1 %copy-start.2 = (bf16[512,256]{1,0:T(8,128)(2,1)S(1)}, bf16[512,256]{1,0:T(8,128)(2,1)}, u32[]{:S(2)}) copy-start(bf16[512,256]{1,0:T(8,128)(2,1)} %constant.8.clone.fh) | copy-start | bytes 786436
  14.6 3.1 %copy-start.3 = (bf16[256,512]{1,0:T(8,128)(2,1)S(1)}, bf16[256,512]{1,0:T(8,128)(2,1)}, u32[]{:S(2)}) copy-start(bf16[256,512]{1,0:T(8,128)(2,1)} %constant.11.clone.il) | copy-start | bytes 786436
  14.6 3.1 %copy-start.4 = (bf16[256,512]{1,0:T(8,128)(2,1)S(1)}, bf16[256,512]{1,0:T(8,128)(2,1)}, u32[]{:S(2)}) copy-start(bf16[256,512]{1,0:T(8,128)(2,1)} %constant.10.clone.ih) | copy-start | bytes 786436
  17.7 22.2 %copy-start.5 = (s32[512]{0:T(512)S(1)}, s32[512]{0:T(512)}, u32[]{:S(2)}) copy-start(s32[512]{0:T(512)} %param.8) | copy-start | bytes 6148

commit v4 on v3

--- a/solution.py
+++ b/solution.py
@@ -142,7 +142,8 @@
 def middle_kernel(valid_ref, near, across, early, before, fh, fl, spec, power):
     base, pair, c = position()
     valid = valid_ref[0]
-    beside = jnp.where(pair == 0, base + GROUP, base - 1)
+    blocks = lax.axis_size("tm")
+    beside = jnp.where(pair == 0, base + GROUP, jnp.where(base == 0, blocks, base - 1))
     transform(near, spec, 1, beside, valid, fh, fl)
     transform(across, spec, 0, base + 2 * (1 - pair) + c, valid, fh, fl)
     for case in range(GROUP):
@@ -247,8 +248,8 @@
         cost_estimate=cost(2 * 3 * FRAMES * LANES * 2),
         name="edge",
     )(own, core)
-    hops = [(s, s - GROUP if s % GROUP < 2 else s + GROUP) for s in range(count)]
-    near = lax.ppermute(edge, "tm", [(s, d) for s, d in hops if 0 <= d < count])
+    hops = [(s, (s - GROUP if s % GROUP < 2 else s + GROUP) % count) for s in range(count)]
+    near = lax.ppermute(edge, "tm", hops)
 
     (fh, fl), (ih, il) = tables()
     early, before = pl.pallas_call(

time: 49.9 us -> 49.1 us (0.984)
  blocking collectives: 30 us -> 25.7 us
  waiting for transfers between devices: 1.93 us -> 4.97 us
    ppermute x1, starting transfers between devices: 1.29 us -> 5.62 us  [body(): near = lax.ppermute(edge, 'tm', hops)]
    all_to_all x1, blocking collectives: 20.9 us -> 16.7 us  [body(): lax.all_to_all(lag_sums.reshape(count, per, LANES), 'tm', 0, 0, tiled=True)]
    ppermute x3, starting transfers between devices: 8.25 us -> 4.36 us  [swapped(): return lax.ppermute(piece, 'tm', [(s, s ^ k) for s in range(count)])]
    ppermute x3, waiting for transfers between devices: 1.62 us -> 3.88 us  [swapped(): return lax.ppermute(piece, 'tm', [(s, s ^ k) for s in range(count)])]
    ppermute x1, waiting for transfers between devices: 0.31 us -> 1.08 us  [body(): near = lax.ppermute(edge, 'tm', hops)]
where the time goes in v4:
time: 49.1 us; the launch traced here: 48.8 us
  blocking collectives  25.7 us (52%)
  starting transfers between devices  9.98 us (20%)
  Pallas kernels  5.85 us (12%)
  waiting for transfers between devices  4.97 us (10%)
  between operations  1.39 us (3%)
  local copies, waits for them, and re-layouts  0.98 us (2%)
    all_to_all x1, blocking collectives, body(): lax.all_to_all(lag_sums.reshape(count, per, LANES), 'tm', 0, 0, tiled=True)  16.7 us
    all_to_all x1, blocking collectives, body(): everyone = lax.all_to_all(sums, 'comp', 0, 0, tiled=True)  9.01 us
    ppermute x1, starting transfers between devices, body(): near = lax.ppermute(edge, 'tm', hops)  5.62 us
    ppermute x3, starting transfers between devices, swapped(): return lax.ppermute(piece, 'tm', [(s, s ^ k) for s in range(count)])  4.36 us
    ppermute x3, waiting for transfers between devices, swapped(): return lax.ppermute(piece, 'tm', [(s, s ^ k) for s in range(count)])  3.88 us
    pallas_call x1, Pallas kernels, body(): pl.pallas_call(functools.partial(pieces_kernel, order), out_shape=(block,...  1.32 us
    pallas_call x1, Pallas kernels, body(): pl.pallas_call(late_kernel, out_shape=f32(LAGS, LANES), in_specs=[smem] +...  1.28 us
    pallas_call x1, Pallas kernels, body(): pl.pallas_call(early_kernel, out_shape=(f32(2, SIZE, 3 * LANES), f32(SIZE...  1.16 us
  transfers between devices with their start and end apart: 4, of which 2 were waited for; matrix products, arithmetic and copies ran while one was open for 0% of the time, Pallas kernels for 5%

profile of v4, /device:TPU:1, one launch (start us, length us, event | category | flops | bytes accessed | tf_op | source)
XLA Modules:
  0.0 48.8 jit_solution(6447110118635299844)
XLA Ops:
  0.6 0.0 copy-start
  0.6 1.3 %pieces.1 = (bf16[3,256,128]{2,1,0:T(8,128)(2,1)S(1)}, bf16[3,256,128]{2,1,0:T(8,128)(2,1)S(1)}, bf16[3,256,128]{2,1,0:T(8,128)(2,1)S(1)}, bf16[3,256,128]{2,1,0:T(8,128)(2,1)S(1)}) custom-call(bf16[3,256,512]{2,1,0:T(8,128)(2,1)} %bitcast.6), custom_call_target="tpu_custom_call" | custom-call | tf_op jit(solution)/shard_map/pieces/pallas_call | solution.py:228
  2.0 3.3 %collective-permute-start.1 = (bf16[3,256,128]{2,1,0:T(8,128)(2,1)S(1)}, bf16[3,256,128]{2,1,0:T(8,128)(2,1)S(1)}, u32[]{:S(2)}, u32[]{:S(2)}) collective-permute-start(bf16[3,256,128]{2,1,0:T(8,128)(2,1)S(1)} %get-tuple-element.12), channel_id=1, source_target_pairs={{0,8},{8,0},{16,24},{24,16},{32,40},{40,32},{48,56},{56,48},{64,72... | collective-permute-start | bytes 589832 | tf_op jit(solution)/shard_map/ppermute | solution.py:239
  5.3 1.0 %collective-permute-start.3 = (bf16[3,256,128]{2,1,0:T(8,128)(2,1)S(1)}, bf16[3,256,128]{2,1,0:T(8,128)(2,1)S(1)}, u32[]{:S(2)}, u32[]{:S(2)}) collective-permute-start(bf16[3,256,128]{2,1,0:T(8,128)(2,1)S(1)} %get-tuple-element.14), channel_id=1, source_target_pairs={{0,16},{8,24},{16,0},{24,8},{32,48},{40,56},{48,32},{56,40},{64,80... | collective-permute-start | bytes 589832 | tf_op jit(solution)/shard_map/ppermute | solution.py:239
  6.3 0.0 collective-permute-done.1.core
  6.4 0.2 edge.1
  6.6 5.6 %collective-permute-start.2 = (bf16[3,256,128]{2,1,0:T(8,128)(2,1)S(1)}, bf16[3,256,128]{2,1,0:T(8,128)(2,1)S(1)}, u32[]{:S(2)}, u32[]{:S(2)}) collective-permute-start(bf16[3,256,128]{2,1,0:T(8,128)(2,1)S(1)} %edge.1), channel_id=1, source_target_pairs={{0,224},{8,232},{16,48},{24,56},{32,0},{40,8},{48,80},{56,88},{64,... | collective-permute-start | bytes 589832 | tf_op jit(solution)/shard_map/ppermute | solution.py:252
  12.2 0.0 collective-permute-start
  12.9 0.0 copy-start.1
  12.9 0.9 %copy-done.1 = bf16[512,256]{1,0:T(8,128)(2,1)S(1)} copy-done((bf16[512,256]{1,0:T(8,128)(2,1)S(1)}, bf16[512,256]{1,0:T(8,128)(2,1)}, u32[]{:S(2)}) %copy-start.1) | copy-done | bytes 262168
  13.8 1.2 %early_blocks.1 = (f32[2,512,384]{2,1,0:T(8,128)S(1)}, f32[512,128]{1,0:T(8,128)S(1)}) custom-call(s32[1]{0:T(128)S(6)} %copy.9.valid_ref, bf16[3,256,128]{2,1,0:T(8,128)(2,1)S(1)} %get-tuple-element.11.own, bf16[3,256,128]{2,1,0:T(8,128)(2,1)S(1)} %collective-permute-done.1.core, bf16[512,256]{1,0:T(8,128)(2,1)S(1)} %copy-done.1, bf16[512,256]{1,0:T(8,128)(2,1)S(1)} %copy-done), custom_call_target="tpu_custom_call" | custom-call | bytes 8000000 | tf_op jit(solution)/shard_map/early_blocks/pallas_call | solution.py:255
  15.0 0.0 copy-start.2
  15.0 0.0 copy-start.3
  15.0 0.0 copy-start.4
  15.0 0.0 collective-permute-done.3.across
  15.1 1.1 %collective-permute-done.2.near = bf16[3,256,128]{2,1,0:T(8,128)(2,1)S(1)} collective-permute-done((bf16[3,256,128]{2,1,0:T(8,128)(2,1)S(1)}, bf16[3,256,128]{2,1,0:T(8,128)(2,1)S(1)}, u32[]{:S(2)}, u32[]{:S(2)}) %collective-permute-start.2) | collective-permute-done | bytes 196640 | tf_op jit(solution)/shard_map/ppermute | solution.py:252
  16.1 1.1 %middle_block.1 = (f32[2,512,384]{2,1,0:T(8,128)S(1)}, f32[512,128]{1,0:T(8,128)S(1)}) custom-call(s32[1]{0:T(128)S(6)} %copy.9.valid_ref, bf16[3,256,128]{2,1,0:T(8,128)(2,1)S(1)} %collective-permute-done.2.near, bf16[3,256,128]{2,1,0:T(8,128)(2,1)S(1)} %collective-permute-done.3.across, f32[2,512,384]{2,1,0:T(8,128)S(1)} %get-tuple-element.13.early, ...), custom_call_target="tpu_custom_call" | custom-call | tf_op jit(solution)/shard_map/middle_block/pallas_call | solution.py:264
  17.3 3.8 %collective-permute-done.corner = bf16[3,256,128]{2,1,0:T(8,128)(2,1)S(1)} collective-permute-done((bf16[3,256,128]{2,1,0:T(8,128)(2,1)S(1)}, bf16[3,256,128]{2,1,0:T(8,128)(2,1)S(1)}, u32[]{:S(2)}, u32[]{:S(2)}) %collective-permute-start) | collective-permute-done | bytes 196640 | tf_op jit(solution)/shard_map/ppermute | solution.py:239
  21.1 0.0 copy-start.5
  21.1 1.3 %lag_sums.1 = f32[256,128]{1,0:T(8,128)S(1)} custom-call(s32[1]{0:T(128)S(6)} %copy.9.valid_ref, bf16[3,256,128]{2,1,0:T(8,128)(2,1)S(1)} %collective-permute-done.corner, f32[2,512,384]{2,1,0:T(8,128)S(1)} %get-tuple-element.13.early, f32[2,512,384]{2,1,0:T(8,128)S(1)} %get-tuple-element.16.middle, f32[512,128]{1,0:T(8,128)S(1)} %get-tuple-element.17.before, ...), custom_call_target="tpu_custom_call" | custom-call | tf_op jit(solution)/shard_map/lag_sums/pallas_call | solution.py:272
  22.4 16.7 %all_to_all.10.parts = f32[32,8,128]{2,1,0:T(8,128)S(1)} all-to-all(f32[32,8,128]{2,1,0:T(8,128)S(1)} %bitcast.3), channel_id=1, replica_groups=mesh['tm'=32,'comp'=8] {'tm'}, dimensions={0} | all-to-all | bytes 262144 | tf_op jit(solution)/shard_map/all_to_all | solution.py:285
  39.1 0.1 sums.1
  39.2 9.0 %all_to_all.11.everyone = f32[8,1,128]{2,1,0:T(1,128)S(1)} all-to-all(f32[8,1,128]{2,1,0:T(1,128)S(1)} %sums.1), channel_id=1, replica_groups=mesh['tm'=32,'comp'=8] {'comp'}, dimensions={0} | all-to-all | bytes 8192 | tf_op jit(solution)/shard_map/all_to_all | solution.py:297
  48.2 0.6 %finish.1 = (f32[8,512]{1,0:T(8,128)}, f32[8]{0:T(128)}) custom-call(s32[1]{0:T(128)S(6)} %copy.9.valid_ref, s32[1,512]{1,0:T(1,128)S(1)} %bitcast.5, f32[32,8,128]{2,1,0:T(8,128)S(1)} %all_to_all.10.parts, f32[8,1,128]{2,1,0:T(1,128)S(1)} %all_to_all.11.everyone), custom_call_target="tpu_custom_call" | custom-call | tf_op jit(solution)/shard_map/finish/pallas_call | solution.py:298
  (5 shorter events, 0.0 us)
Async XLA Ops:
  0.6 12.2 %copy-start = (bf16[512,256]{1,0:T(8,128)(2,1)S(1)}, bf16[512,256]{1,0:T(8,128)(2,1)}, u32[]{:S(2)}) copy-start(bf16[512,256]{1,0:T(8,128)(2,1)} %constant.9.clone.fl) | copy-start | bytes 786436
  2.0 4.4 %collective-permute-start.1 = (bf16[3,256,128]{2,1,0:T(8,128)(2,1)S(1)}, bf16[3,256,128]{2,1,0:T(8,128)(2,1)S(1)}, u32[]{:S(2)}, u32[]{:S(2)}) collective-permute-start(bf16[3,256,128]{2,1,0:T(8,128)(2,1)S(1)} %get-tuple-element.12), channel_id=1, source_target_pairs={{0,8},{8,0},{16,24},{24,16},{32,40},{40,32},{48,56},{56,48},{64,72... | collective-permute-start | bytes 589832 | tf_op jit(solution)/shard_map/ppermute | solution.py:239
  5.3 9.8 %collective-permute-start.3 = (bf16[3,256,128]{2,1,0:T(8,128)(2,1)S(1)}, bf16[3,256,128]{2,1,0:T(8,128)(2,1)S(1)}, u32[]{:S(2)}, u32[]{:S(2)}) collective-permute-start(bf16[3,256,128]{2,1,0:T(8,128)(2,1)S(1)} %get-tuple-element.14), channel_id=1, source_target_pairs={{0,16},{8,24},{16,0},{24,8},{32,48},{40,56},{48,32},{56,40},{64,80... | collective-permute-start | bytes 589832 | tf_op jit(solution)/shard_map/ppermute | solution.py:239
  6.6 9.5 %collective-permute-start.2 = (bf16[3,256,128]{2,1,0:T(8,128)(2,1)S(1)}, bf16[3,256,128]{2,1,0:T(8,128)(2,1)S(1)}, u32[]{:S(2)}, u32[]{:S(2)}) collective-permute-start(bf16[3,256,128]{2,1,0:T(8,128)(2,1)S(1)} %edge.1), channel_id=1, source_target_pairs={{0,224},{8,232},{16,48},{24,56},{32,0},{40,8},{48,80},{56,88},{64,... | collective-permute-start | bytes 589832 | tf_op jit(solution)/shard_map/ppermute | solution.py:252
  12.2 8.9 %collective-permute-start = (bf16[3,256,128]{2,1,0:T(8,128)(2,1)S(1)}, bf16[3,256,128]{2,1,0:T(8,128)(2,1)S(1)}, u32[]{:S(2)}, u32[]{:S(2)}) collective-permute-start(bf16[3,256,128]{2,1,0:T(8,128)(2,1)S(1)} %get-tuple-element.10), channel_id=1, source_target_pairs={{0,24},{8,16},{16,8},{24,0},{32,56},{40,48},{48,40},{56,32},{64,88... | collective-permute-start | bytes 589832 | tf_op jit(solution)/shard_map/ppermute | solution.py:239
  12.9 1.0 %copy-start.1 = (bf16[512,256]{1,0:T(8,128)(2,1)S(1)}, bf16[512,256]{1,0:T(8,128)(2,1)}, u32[]{:S(2)}) copy-start(bf16[512,256]{1,0:T(8,128)(2,1)} %constant.8.clone.fh) | copy-start | bytes 786436
  15.0 6.1 %copy-start.2 = (bf16[512,256]{1,0:T(8,128)(2,1)S(1)}, bf16[512,256]{1,0:T(8,128)(2,1)}, u32[]{:S(2)}) copy-start(bf16[512,256]{1,0:T(8,128)(2,1)} %constant.8.clone.fh) | copy-start | bytes 786436
  15.0 6.1 %copy-start.3 = (bf16[256,512]{1,0:T(8,128)(2,1)S(1)}, bf16[256,512]{1,0:T(8,128)(2,1)}, u32[]{:S(2)}) copy-start(bf16[256,512]{1,0:T(8,128)(2,1)} %constant.11.clone.il) | copy-start | bytes 786436
  15.0 6.1 %copy-start.4 = (bf16[256,512]{1,0:T(8,128)(2,1)S(1)}, bf16[256,512]{1,0:T(8,128)(2,1)}, u32[]{:S(2)}) copy-start(bf16[256,512]{1,0:T(8,128)(2,1)} %constant.10.clone.ih) | copy-start | bytes 786436
  21.1 18.0 %copy-start.5 = (s32[512]{0:T(512)S(1)}, s32[512]{0:T(512)}, u32[]{:S(2)}) copy-start(s32[512]{0:T(512)} %param.8) | copy-start | bytes 6148

commit v5 on v4

--- a/solution.py
+++ b/solution.py
@@ -22,12 +22,13 @@
     return high, low
 
 
-def tables():
+def tables(order, per):
     f = np.concatenate([np.arange(0, SIZE // 2, 2), np.arange(1, SIZE // 2, 2)])
     angle = 2.0 * np.pi * (f + 0.5) / SIZE
     ahead = angle[:, None] * np.arange(FRAMES)[None, :]
     forward = np.concatenate([np.cos(ahead), -np.sin(ahead)], 0)
-    back = angle[None, :] * np.arange(LAGS)[:, None]
+    lags = np.concatenate([np.arange(t * per, (t + 1) * per) for t in order])
+    back = angle[None, :] * lags[:, None]
     inverse = np.concatenate([np.cos(back), -np.sin(back)], 1) * (2.0 / SIZE)
     return two_parts(forward), two_parts(inverse)
 
@@ -55,7 +56,7 @@
     into[slot] = dot(fh[...], clean) + dot(fl[...], clean)
 
 
-def products(power, before, blocks, alone, pairs, rows=8):
+def products(power, before, blocks, alone, pairs, rows=32):
     half = SIZE // 2
     for parity in range(2):
 
@@ -174,23 +175,21 @@
     out[...] = both[:, :LANES] + (dot(il[...], ph) + both[:, LANES:])
 
 
-def correlations(valid_ref, mask_ref, parts):
+def correlations(order, valid_ref, mask_ref, parts):
     per = parts.shape[1]
     lag = lax.axis_index("tm") * per + lax.broadcasted_iota(jnp.int32, (per, LANES), 0)
     anchors = (valid_ref[0] - lag).astype(jnp.float32)
     for q in range(GROUP):
-        lag_sum = parts[q]
-        for z in range(1, parts.shape[0] // GROUP):
-            lag_sum = lag_sum + parts[z * GROUP + q]
+        lag_sum = sum(parts[k] for k, source in enumerate(order) if source % GROUP == q)
         weight = mask_ref[:, q * LANES : (q + 1) * LANES].astype(jnp.float32)
         yield q, weight, weight * lag_sum / anchors
 
 
-def sums_kernel(valid_ref, mask_ref, parts, sums):
+def sums_kernel(order, valid_ref, mask_ref, parts, sums):
     per = parts.shape[1]
     total = jnp.zeros((per, LANES), jnp.float32)
     count = jnp.zeros((1, LANES), jnp.float32)
-    for _, weight, value in correlations(valid_ref, mask_ref, parts):
+    for _, weight, value in correlations(order, valid_ref, mask_ref, parts):
         total = total + value
         count = count + weight
     row = jnp.sum(total, axis=1, keepdims=True)
@@ -202,8 +201,8 @@
     sums[...] = jnp.broadcast_to(line[None], sums.shape)
 
 
-def finish_kernel(valid_ref, mask_ref, parts, everyone, corr, average):
-    for q, _, value in correlations(valid_ref, mask_ref, parts):
+def finish_kernel(order, valid_ref, mask_ref, parts, everyone, corr, average):
+    for q, _, value in correlations(order, valid_ref, mask_ref, parts):
         corr[:, q * LANES : (q + 1) * LANES] = value
     line = jnp.sum(everyone[...], axis=0)
     lane = lax.broadcasted_iota(jnp.int32, line.shape, 1)
@@ -251,7 +250,8 @@
     hops = [(s, (s - GROUP if s % GROUP < 2 else s + GROUP) % count) for s in range(count)]
     near = lax.ppermute(edge, "tm", hops)
 
-    (fh, fl), (ih, il) = tables()
+    order = list(range(count))[::-1]
+    (fh, fl), (ih, il) = tables(order, per)
     early, before = pl.pallas_call(
         early_kernel,
         out_shape=(f32(2, SIZE, 3 * LANES), f32(SIZE, LANES)),
@@ -283,20 +283,27 @@
     )(valid_frames, corner, early, middle, before, fh, fl, ih, il)
 
     parts = lax.all_to_all(
-        lag_sums.reshape(count, per, LANES), "tm", 0, 0, tiled=True
+        lag_sums.reshape(count, per, LANES),
+        "tm",
+        0,
+        0,
+        tiled=True,
+        axis_index_groups=[order],
     )
     mask = atom_mask.reshape(1, atoms)
     sums = pl.pallas_call(
-        sums_kernel,
+        functools.partial(sums_kernel, order),
         out_shape=f32(comps, 1, LANES),
         in_specs=[smem, vmem, vmem],
         out_specs=vmem,
         compiler_params=params(2),
         name="sums",
     )(valid_frames, mask, parts)
-    everyone = lax.all_to_all(sums, "comp", 0, 0, tiled=True)
+    everyone = lax.all_to_all(
+        sums, "comp", 0, 0, tiled=True, axis_index_groups=[list(range(comps))[::-1]]
+    )
     correlation, average = pl.pallas_call(
-        finish_kernel,
+        functools.partial(finish_kernel, order),
         out_shape=(f32(per, atoms), f32(per)),
         in_specs=[smem, vmem, vmem, vmem],
         out_specs=(vmem, vmem),

time: 49.1 us -> 44.8 us (0.912)
  blocking collectives: 25.7 us -> 21.1 us
  Pallas kernels: 5.85 us -> 5.32 us
    all_to_all x2, blocking collectives: 25.7 us -> 21.1 us  [the longest x1 13.1 us: body(): lax.all_to_all(lag_sums.reshape(count, per, LANES), 'tm', 0, 0, tiled=Tru...]
where the time goes in v5:
time: 44.8 us; the launch traced here: 44.1 us
  blocking collectives  21.1 us (47%)
  starting transfers between devices  9.98 us (22%)
  waiting for transfers between devices  5.34 us (12%)
  Pallas kernels  5.32 us (12%)
  between operations  1.39 us (3%)
  local copies, waits for them, and re-layouts  0.98 us (2%)
    all_to_all x1, blocking collectives, body(): lax.all_to_all(lag_sums.reshape(count, per, LANES), 'tm', 0, 0, tiled=Tru...  13.1 us
    all_to_all x1, blocking collectives, body(): lax.all_to_all(sums, 'comp', 0, 0, tiled=True, axis_index_groups=[list(ra...  8.01 us
    ppermute x1, starting transfers between devices, body(): near = lax.ppermute(edge, 'tm', hops)  5.62 us
    ppermute x3, starting transfers between devices, swapped(): return lax.ppermute(piece, 'tm', [(s, s ^ k) for s in range(count)])  4.36 us
    ppermute x3, waiting for transfers between devices, swapped(): return lax.ppermute(piece, 'tm', [(s, s ^ k) for s in range(count)])  4.07 us
    pallas_call x1, Pallas kernels, body(): pl.pallas_call(functools.partial(pieces_kernel, order), out_shape=(block,...  1.32 us
    ppermute x1, waiting for transfers between devices, body(): near = lax.ppermute(edge, 'tm', hops)  1.27 us
    pallas_call x1, Pallas kernels, body(): pl.pallas_call(late_kernel, out_shape=f32(LAGS, LANES), in_specs=[smem] +...  1.12 us
  transfers between devices with their start and end apart: 4, of which 2 were waited for; matrix products, arithmetic and copies ran while one was open for 0% of the time, Pallas kernels for 5%

profile of v5, /device:TPU:1, one launch (start us, length us, event | category | flops | bytes accessed | tf_op | source)
XLA Modules:
  0.0 44.1 jit_solution(5587620532545600172)
XLA Ops:
  0.6 0.0 copy-start
  0.6 1.3 %pieces.1 = (bf16[3,256,128]{2,1,0:T(8,128)(2,1)S(1)}, bf16[3,256,128]{2,1,0:T(8,128)(2,1)S(1)}, bf16[3,256,128]{2,1,0:T(8,128)(2,1)S(1)}, bf16[3,256,128]{2,1,0:T(8,128)(2,1)S(1)}) custom-call(bf16[3,256,512]{2,1,0:T(8,128)(2,1)} %bitcast.6), custom_call_target="tpu_custom_call" | custom-call | tf_op jit(solution)/shard_map/pieces/pallas_call | solution.py:227
  2.0 3.3 %collective-permute-start.1 = (bf16[3,256,128]{2,1,0:T(8,128)(2,1)S(1)}, bf16[3,256,128]{2,1,0:T(8,128)(2,1)S(1)}, u32[]{:S(2)}, u32[]{:S(2)}) collective-permute-start(bf16[3,256,128]{2,1,0:T(8,128)(2,1)S(1)} %get-tuple-element.12), channel_id=1, source_target_pairs={{0,8},{8,0},{16,24},{24,16},{32,40},{40,32},{48,56},{56,48},{64,72... | collective-permute-start | bytes 589832 | tf_op jit(solution)/shard_map/ppermute | solution.py:238
  5.3 1.0 %collective-permute-start.3 = (bf16[3,256,128]{2,1,0:T(8,128)(2,1)S(1)}, bf16[3,256,128]{2,1,0:T(8,128)(2,1)S(1)}, u32[]{:S(2)}, u32[]{:S(2)}) collective-permute-start(bf16[3,256,128]{2,1,0:T(8,128)(2,1)S(1)} %get-tuple-element.14), channel_id=1, source_target_pairs={{0,16},{8,24},{16,0},{24,8},{32,48},{40,56},{48,32},{56,40},{64,80... | collective-permute-start | bytes 589832 | tf_op jit(solution)/shard_map/ppermute | solution.py:238
  6.3 0.0 collective-permute-done.1.core
  6.4 0.2 edge.1
  6.6 5.6 %collective-permute-start.2 = (bf16[3,256,128]{2,1,0:T(8,128)(2,1)S(1)}, bf16[3,256,128]{2,1,0:T(8,128)(2,1)S(1)}, u32[]{:S(2)}, u32[]{:S(2)}) collective-permute-start(bf16[3,256,128]{2,1,0:T(8,128)(2,1)S(1)} %edge.1), channel_id=1, source_target_pairs={{0,224},{8,232},{16,48},{24,56},{32,0},{40,8},{48,80},{56,88},{64,... | collective-permute-start | bytes 589832 | tf_op jit(solution)/shard_map/ppermute | solution.py:251
  12.2 0.0 collective-permute-start
  12.9 0.0 copy-start.1
  12.9 0.9 %copy-done.1 = bf16[512,256]{1,0:T(8,128)(2,1)S(1)} copy-done((bf16[512,256]{1,0:T(8,128)(2,1)S(1)}, bf16[512,256]{1,0:T(8,128)(2,1)}, u32[]{:S(2)}) %copy-start.1) | copy-done | bytes 262168
  13.8 1.0 %early_blocks.1 = (f32[2,512,384]{2,1,0:T(8,128)S(1)}, f32[512,128]{1,0:T(8,128)S(1)}) custom-call(s32[1]{0:T(128)S(6)} %copy.9.valid_ref, bf16[3,256,128]{2,1,0:T(8,128)(2,1)S(1)} %get-tuple-element.11.own, bf16[3,256,128]{2,1,0:T(8,128)(2,1)S(1)} %collective-permute-done.1.core, bf16[512,256]{1,0:T(8,128)(2,1)S(1)} %copy-done.1, bf16[512,256]{1,0:T(8,128)(2,1)S(1)} %copy-done), custom_call_target="tpu_custom_call" | custom-call | bytes 8000000 | tf_op jit(solution)/shard_map/early_blocks/pallas_call | solution.py:255
  14.8 0.0 copy-start.2
  14.8 0.0 copy-start.3
  14.8 0.0 copy-start.4
  14.9 0.0 collective-permute-done.3.across
  14.9 1.3 %collective-permute-done.2.near = bf16[3,256,128]{2,1,0:T(8,128)(2,1)S(1)} collective-permute-done((bf16[3,256,128]{2,1,0:T(8,128)(2,1)S(1)}, bf16[3,256,128]{2,1,0:T(8,128)(2,1)S(1)}, u32[]{:S(2)}, u32[]{:S(2)}) %collective-permute-start.2) | collective-permute-done | bytes 196640 | tf_op jit(solution)/shard_map/ppermute | solution.py:251
  16.1 1.0 %middle_block.1 = (f32[2,512,384]{2,1,0:T(8,128)S(1)}, f32[512,128]{1,0:T(8,128)S(1)}) custom-call(s32[1]{0:T(128)S(6)} %copy.9.valid_ref, bf16[3,256,128]{2,1,0:T(8,128)(2,1)S(1)} %collective-permute-done.2.near, bf16[3,256,128]{2,1,0:T(8,128)(2,1)S(1)} %collective-permute-done.3.across, f32[2,512,384]{2,1,0:T(8,128)S(1)} %get-tuple-element.13.early, ...), custom_call_target="tpu_custom_call" | custom-call | tf_op jit(solution)/shard_map/middle_block/pallas_call | solution.py:264
  17.1 4.0 %collective-permute-done.corner = bf16[3,256,128]{2,1,0:T(8,128)(2,1)S(1)} collective-permute-done((bf16[3,256,128]{2,1,0:T(8,128)(2,1)S(1)}, bf16[3,256,128]{2,1,0:T(8,128)(2,1)S(1)}, u32[]{:S(2)}, u32[]{:S(2)}) %collective-permute-start) | collective-permute-done | bytes 196640 | tf_op jit(solution)/shard_map/ppermute | solution.py:238
  21.1 0.0 copy-start.5
  21.1 1.1 %lag_sums.1 = f32[256,128]{1,0:T(8,128)S(1)} custom-call(s32[1]{0:T(128)S(6)} %copy.9.valid_ref, bf16[3,256,128]{2,1,0:T(8,128)(2,1)S(1)} %collective-permute-done.corner, f32[2,512,384]{2,1,0:T(8,128)S(1)} %get-tuple-element.13.early, f32[2,512,384]{2,1,0:T(8,128)S(1)} %get-tuple-element.16.middle, f32[512,128]{1,0:T(8,128)S(1)} %get-tuple-element.17.before, ...), custom_call_target="tpu_custom_call" | custom-call | tf_op jit(solution)/shard_map/lag_sums/pallas_call | solution.py:272
  22.3 13.1 %all_to_all.10.parts = f32[32,8,128]{2,1,0:T(8,128)S(1)} all-to-all(f32[32,8,128]{2,1,0:T(8,128)S(1)} %bitcast.3), channel_id=1, replica_groups={{248,240,232,224,216,208,200,192,184,176,168,160,152,144,136,128,120,11..., dimensions={0} | all-to-all | bytes 262144 | tf_op jit(solution)/shard_map/all_to_all | solution.py:285
  35.4 0.1 sums.1
  35.5 8.0 %all_to_all.11.everyone = f32[8,1,128]{2,1,0:T(1,128)S(1)} all-to-all(f32[8,1,128]{2,1,0:T(1,128)S(1)} %sums.1), channel_id=1, replica_groups={{7,6,5,4,3,2,1,0},{15,14,13,12,11,10,9,8},{23,22,21,20,19,18,17,16},{31..., dimensions={0} | all-to-all | bytes 8192 | tf_op jit(solution)/shard_map/all_to_all | solution.py:302
  43.5 0.6 %finish.1 = (f32[8,512]{1,0:T(8,128)}, f32[8]{0:T(128)}) custom-call(s32[1]{0:T(128)S(6)} %copy.9.valid_ref, s32[1,512]{1,0:T(1,128)S(1)} %bitcast.5, f32[32,8,128]{2,1,0:T(8,128)S(1)} %all_to_all.10.parts, f32[8,1,128]{2,1,0:T(1,128)S(1)} %all_to_all.11.everyone), custom_call_target="tpu_custom_call" | custom-call | tf_op jit(solution)/shard_map/finish/pallas_call | solution.py:305
  (5 shorter events, 0.0 us)
Async XLA Ops:
  0.6 12.2 %copy-start = (bf16[512,256]{1,0:T(8,128)(2,1)S(1)}, bf16[512,256]{1,0:T(8,128)(2,1)}, u32[]{:S(2)}) copy-start(bf16[512,256]{1,0:T(8,128)(2,1)} %constant.9.clone.fl) | copy-start | bytes 786436
  2.0 4.4 %collective-permute-start.1 = (bf16[3,256,128]{2,1,0:T(8,128)(2,1)S(1)}, bf16[3,256,128]{2,1,0:T(8,128)(2,1)S(1)}, u32[]{:S(2)}, u32[]{:S(2)}) collective-permute-start(bf16[3,256,128]{2,1,0:T(8,128)(2,1)S(1)} %get-tuple-element.12), channel_id=1, source_target_pairs={{0,8},{8,0},{16,24},{24,16},{32,40},{40,32},{48,56},{56,48},{64,72... | collective-permute-start | bytes 589832 | tf_op jit(solution)/shard_map/ppermute | solution.py:238
  5.3 9.6 %collective-permute-start.3 = (bf16[3,256,128]{2,1,0:T(8,128)(2,1)S(1)}, bf16[3,256,128]{2,1,0:T(8,128)(2,1)S(1)}, u32[]{:S(2)}, u32[]{:S(2)}) collective-permute-start(bf16[3,256,128]{2,1,0:T(8,128)(2,1)S(1)} %get-tuple-element.14), channel_id=1, source_target_pairs={{0,16},{8,24},{16,0},{24,8},{32,48},{40,56},{48,32},{56,40},{64,80... | collective-permute-start | bytes 589832 | tf_op jit(solution)/shard_map/ppermute | solution.py:238
  6.6 9.5 %collective-permute-start.2 = (bf16[3,256,128]{2,1,0:T(8,128)(2,1)S(1)}, bf16[3,256,128]{2,1,0:T(8,128)(2,1)S(1)}, u32[]{:S(2)}, u32[]{:S(2)}) collective-permute-start(bf16[3,256,128]{2,1,0:T(8,128)(2,1)S(1)} %edge.1), channel_id=1, source_target_pairs={{0,224},{8,232},{16,48},{24,56},{32,0},{40,8},{48,80},{56,88},{64,... | collective-permute-start | bytes 589832 | tf_op jit(solution)/shard_map/ppermute | solution.py:251
  12.2 8.9 %collective-permute-start = (bf16[3,256,128]{2,1,0:T(8,128)(2,1)S(1)}, bf16[3,256,128]{2,1,0:T(8,128)(2,1)S(1)}, u32[]{:S(2)}, u32[]{:S(2)}) collective-permute-start(bf16[3,256,128]{2,1,0:T(8,128)(2,1)S(1)} %get-tuple-element.10), channel_id=1, source_target_pairs={{0,24},{8,16},{16,8},{24,0},{32,56},{40,48},{48,40},{56,32},{64,88... | collective-permute-start | bytes 589832 | tf_op jit(solution)/shard_map/ppermute | solution.py:238
  12.9 1.0 %copy-start.1 = (bf16[512,256]{1,0:T(8,128)(2,1)S(1)}, bf16[512,256]{1,0:T(8,128)(2,1)}, u32[]{:S(2)}) copy-start(bf16[512,256]{1,0:T(8,128)(2,1)} %constant.8.clone.fh) | copy-start | bytes 786436
  14.8 6.3 %copy-start.2 = (bf16[512,256]{1,0:T(8,128)(2,1)S(1)}, bf16[512,256]{1,0:T(8,128)(2,1)}, u32[]{:S(2)}) copy-start(bf16[512,256]{1,0:T(8,128)(2,1)} %constant.8.clone.fh) | copy-start | bytes 786436
  14.8 6.3 %copy-start.3 = (bf16[256,512]{1,0:T(8,128)(2,1)S(1)}, bf16[256,512]{1,0:T(8,128)(2,1)}, u32[]{:S(2)}) copy-start(bf16[256,512]{1,0:T(8,128)(2,1)} %constant.11.clone.il) | copy-start | bytes 786436
  14.8 6.3 %copy-start.4 = (bf16[256,512]{1,0:T(8,128)(2,1)S(1)}, bf16[256,512]{1,0:T(8,128)(2,1)}, u32[]{:S(2)}) copy-start(bf16[256,512]{1,0:T(8,128)(2,1)} %constant.10.clone.ih) | copy-start | bytes 786436
  21.1 14.2 %copy-start.5 = (s32[512]{0:T(512)S(1)}, s32[512]{0:T(512)}, u32[]{:S(2)}) copy-start(s32[512]{0:T(512)} %param.8) | copy-start | bytes 6148

commit v6 on v5

--- a/solution.py
+++ b/solution.py
@@ -250,7 +250,7 @@
     hops = [(s, (s - GROUP if s % GROUP < 2 else s + GROUP) % count) for s in range(count)]
     near = lax.ppermute(edge, "tm", hops)
 
-    order = list(range(count))[::-1]
+    order = [z * GROUP + x * 2 + c for x in (1, 0) for z in range(count // GROUP)[::-1] for c in (1, 0)]
     (fh, fl), (ih, il) = tables(order, per)
     early, before = pl.pallas_call(
         early_kernel,
@@ -300,7 +300,7 @@
         name="sums",
     )(valid_frames, mask, parts)
     everyone = lax.all_to_all(
-        sums, "comp", 0, 0, tiled=True, axis_index_groups=[list(range(comps))[::-1]]
+        sums, "comp", 0, 0, tiled=True, axis_index_groups=[[y * 2 + x for y in (2, 3, 1, 0) for x in (1, 0)]]
     )
     correlation, average = pl.pallas_call(
         functools.partial(finish_kernel, order),

time: 44.8 us -> 43.9 us (0.980); the launches traced: 44.1 us -> 43.7 us
    all_to_all x1, blocking collectives: 8.01 us -> 7.31 us  [body(): lax.all_to_all(sums, 'comp', 0, 0, tiled=True, axis_index_groups=[[y * 2...]
where the time goes in v6:
time: 43.9 us; the launch traced here: 43.7 us
  blocking collectives  20.7 us (47%)
  starting transfers between devices  9.98 us (23%)
  waiting for transfers between devices  5.34 us (12%)
  Pallas kernels  5.31 us (12%)
  between operations  1.39 us (3%)
  local copies, waits for them, and re-layouts  0.98 us (2%)
    all_to_all x1, blocking collectives, body(): lax.all_to_all(lag_sums.reshape(count, per, LANES), 'tm', 0, 0, tiled=Tru...  13.4 us
    all_to_all x1, blocking collectives, body(): lax.all_to_all(sums, 'comp', 0, 0, tiled=True, axis_index_groups=[[y * 2...  7.31 us
    ppermute x1, starting transfers between devices, body(): near = lax.ppermute(edge, 'tm', hops)  5.62 us
    ppermute x3, starting transfers between devices, swapped(): return lax.ppermute(piece, 'tm', [(s, s ^ k) for s in range(count)])  4.36 us
    ppermute x3, waiting for transfers between devices, swapped(): return lax.ppermute(piece, 'tm', [(s, s ^ k) for s in range(count)])  4.07 us
    pallas_call x1, Pallas kernels, body(): pl.pallas_call(functools.partial(pieces_kernel, order), out_shape=(block,...  1.32 us
    ppermute x1, waiting for transfers between devices, body(): near = lax.ppermute(edge, 'tm', hops)  1.27 us
    pallas_call x1, Pallas kernels, body(): pl.pallas_call(late_kernel, out_shape=f32(LAGS, LANES), in_specs=[smem] +...  1.12 us
  transfers between devices with their start and end apart: 4, of which 2 were waited for; matrix products, arithmetic and copies ran while one was open for 0% of the time, Pallas kernels for 5%

profile of v6, /device:TPU:1, one launch (start us, length us, event | category | flops | bytes accessed | tf_op | source)
XLA Modules:
  0.0 43.7 jit_solution(16073116766983711998)
XLA Ops:
  0.6 0.0 copy-start
  0.6 1.3 %pieces.1 = (bf16[3,256,128]{2,1,0:T(8,128)(2,1)S(1)}, bf16[3,256,128]{2,1,0:T(8,128)(2,1)S(1)}, bf16[3,256,128]{2,1,0:T(8,128)(2,1)S(1)}, bf16[3,256,128]{2,1,0:T(8,128)(2,1)S(1)}) custom-call(bf16[3,256,512]{2,1,0:T(8,128)(2,1)} %bitcast.6), custom_call_target="tpu_custom_call" | custom-call | tf_op jit(solution)/shard_map/pieces/pallas_call | solution.py:227
  2.0 3.3 %collective-permute-start.1 = (bf16[3,256,128]{2,1,0:T(8,128)(2,1)S(1)}, bf16[3,256,128]{2,1,0:T(8,128)(2,1)S(1)}, u32[]{:S(2)}, u32[]{:S(2)}) collective-permute-start(bf16[3,256,128]{2,1,0:T(8,128)(2,1)S(1)} %get-tuple-element.12), channel_id=1, source_target_pairs={{0,8},{8,0},{16,24},{24,16},{32,40},{40,32},{48,56},{56,48},{64,72... | collective-permute-start | bytes 589832 | tf_op jit(solution)/shard_map/ppermute | solution.py:238
  5.3 1.0 %collective-permute-start.3 = (bf16[3,256,128]{2,1,0:T(8,128)(2,1)S(1)}, bf16[3,256,128]{2,1,0:T(8,128)(2,1)S(1)}, u32[]{:S(2)}, u32[]{:S(2)}) collective-permute-start(bf16[3,256,128]{2,1,0:T(8,128)(2,1)S(1)} %get-tuple-element.14), channel_id=1, source_target_pairs={{0,16},{8,24},{16,0},{24,8},{32,48},{40,56},{48,32},{56,40},{64,80... | collective-permute-start | bytes 589832 | tf_op jit(solution)/shard_map/ppermute | solution.py:238
  6.3 0.0 collective-permute-done.1.core
  6.4 0.2 edge.1
  6.6 5.6 %collective-permute-start.2 = (bf16[3,256,128]{2,1,0:T(8,128)(2,1)S(1)}, bf16[3,256,128]{2,1,0:T(8,128)(2,1)S(1)}, u32[]{:S(2)}, u32[]{:S(2)}) collective-permute-start(bf16[3,256,128]{2,1,0:T(8,128)(2,1)S(1)} %edge.1), channel_id=1, source_target_pairs={{0,224},{8,232},{16,48},{24,56},{32,0},{40,8},{48,80},{56,88},{64,... | collective-permute-start | bytes 589832 | tf_op jit(solution)/shard_map/ppermute | solution.py:251
  12.2 0.0 collective-permute-start
  12.9 0.0 copy-start.1
  12.9 0.9 %copy-done.1 = bf16[512,256]{1,0:T(8,128)(2,1)S(1)} copy-done((bf16[512,256]{1,0:T(8,128)(2,1)S(1)}, bf16[512,256]{1,0:T(8,128)(2,1)}, u32[]{:S(2)}) %copy-start.1) | copy-done | bytes 262168
  13.8 1.0 %early_blocks.1 = (f32[2,512,384]{2,1,0:T(8,128)S(1)}, f32[512,128]{1,0:T(8,128)S(1)}) custom-call(s32[1]{0:T(128)S(6)} %copy.9.valid_ref, bf16[3,256,128]{2,1,0:T(8,128)(2,1)S(1)} %get-tuple-element.11.own, bf16[3,256,128]{2,1,0:T(8,128)(2,1)S(1)} %collective-permute-done.1.core, bf16[512,256]{1,0:T(8,128)(2,1)S(1)} %copy-done.1, bf16[512,256]{1,0:T(8,128)(2,1)S(1)} %copy-done), custom_call_target="tpu_custom_call" | custom-call | bytes 8000000 | tf_op jit(solution)/shard_map/early_blocks/pallas_call | solution.py:255
  14.8 0.0 copy-start.2
  14.8 0.0 copy-start.3
  14.8 0.0 copy-start.4
  14.9 0.0 collective-permute-done.3.across
  14.9 1.3 %collective-permute-done.2.near = bf16[3,256,128]{2,1,0:T(8,128)(2,1)S(1)} collective-permute-done((bf16[3,256,128]{2,1,0:T(8,128)(2,1)S(1)}, bf16[3,256,128]{2,1,0:T(8,128)(2,1)S(1)}, u32[]{:S(2)}, u32[]{:S(2)}) %collective-permute-start.2) | collective-permute-done | bytes 196640 | tf_op jit(solution)/shard_map/ppermute | solution.py:251
  16.1 1.0 %middle_block.1 = (f32[2,512,384]{2,1,0:T(8,128)S(1)}, f32[512,128]{1,0:T(8,128)S(1)}) custom-call(s32[1]{0:T(128)S(6)} %copy.9.valid_ref, bf16[3,256,128]{2,1,0:T(8,128)(2,1)S(1)} %collective-permute-done.2.near, bf16[3,256,128]{2,1,0:T(8,128)(2,1)S(1)} %collective-permute-done.3.across, f32[2,512,384]{2,1,0:T(8,128)S(1)} %get-tuple-element.13.early, ...), custom_call_target="tpu_custom_call" | custom-call | tf_op jit(solution)/shard_map/middle_block/pallas_call | solution.py:264
  17.1 4.0 %collective-permute-done.corner = bf16[3,256,128]{2,1,0:T(8,128)(2,1)S(1)} collective-permute-done((bf16[3,256,128]{2,1,0:T(8,128)(2,1)S(1)}, bf16[3,256,128]{2,1,0:T(8,128)(2,1)S(1)}, u32[]{:S(2)}, u32[]{:S(2)}) %collective-permute-start) | collective-permute-done | bytes 196640 | tf_op jit(solution)/shard_map/ppermute | solution.py:238
  21.1 0.0 copy-start.5
  21.1 1.1 %lag_sums.1 = f32[256,128]{1,0:T(8,128)S(1)} custom-call(s32[1]{0:T(128)S(6)} %copy.9.valid_ref, bf16[3,256,128]{2,1,0:T(8,128)(2,1)S(1)} %collective-permute-done.corner, f32[2,512,384]{2,1,0:T(8,128)S(1)} %get-tuple-element.13.early, f32[2,512,384]{2,1,0:T(8,128)S(1)} %get-tuple-element.16.middle, f32[512,128]{1,0:T(8,128)S(1)} %get-tuple-element.17.before, ...), custom_call_target="tpu_custom_call" | custom-call | tf_op jit(solution)/shard_map/lag_sums/pallas_call | solution.py:272
  22.3 13.4 %all_to_all.10.parts = f32[32,8,128]{2,1,0:T(8,128)S(1)} all-to-all(f32[32,8,128]{2,1,0:T(8,128)S(1)} %bitcast.3), channel_id=1, replica_groups={{248,240,216,208,184,176,152,144,120,112,88,80,56,48,24,16,232,224,200,..., dimensions={0} | all-to-all | bytes 262144 | tf_op jit(solution)/shard_map/all_to_all | solution.py:285
  35.7 0.1 sums.1
  35.8 7.3 %all_to_all.11.everyone = f32[8,1,128]{2,1,0:T(1,128)S(1)} all-to-all(f32[8,1,128]{2,1,0:T(1,128)S(1)} %sums.1), channel_id=1, replica_groups={{5,4,7,6,3,2,1,0},{13,12,15,14,11,10,9,8},{21,20,23,22,19,18,17,16},{29..., dimensions={0} | all-to-all | bytes 8192 | tf_op jit(solution)/shard_map/all_to_all | solution.py:302
  43.1 0.6 %finish.1 = (f32[8,512]{1,0:T(8,128)}, f32[8]{0:T(128)}) custom-call(s32[1]{0:T(128)S(6)} %copy.9.valid_ref, s32[1,512]{1,0:T(1,128)S(1)} %bitcast.5, f32[32,8,128]{2,1,0:T(8,128)S(1)} %all_to_all.10.parts, f32[8,1,128]{2,1,0:T(1,128)S(1)} %all_to_all.11.everyone), custom_call_target="tpu_custom_call" | custom-call | tf_op jit(solution)/shard_map/finish/pallas_call | solution.py:305
  (5 shorter events, 0.0 us)
Async XLA Ops:
  0.6 12.2 %copy-start = (bf16[512,256]{1,0:T(8,128)(2,1)S(1)}, bf16[512,256]{1,0:T(8,128)(2,1)}, u32[]{:S(2)}) copy-start(bf16[512,256]{1,0:T(8,128)(2,1)} %constant.9.clone.fl) | copy-start | bytes 786436
  2.0 4.4 %collective-permute-start.1 = (bf16[3,256,128]{2,1,0:T(8,128)(2,1)S(1)}, bf16[3,256,128]{2,1,0:T(8,128)(2,1)S(1)}, u32[]{:S(2)}, u32[]{:S(2)}) collective-permute-start(bf16[3,256,128]{2,1,0:T(8,128)(2,1)S(1)} %get-tuple-element.12), channel_id=1, source_target_pairs={{0,8},{8,0},{16,24},{24,16},{32,40},{40,32},{48,56},{56,48},{64,72... | collective-permute-start | bytes 589832 | tf_op jit(solution)/shard_map/ppermute | solution.py:238
  5.3 9.6 %collective-permute-start.3 = (bf16[3,256,128]{2,1,0:T(8,128)(2,1)S(1)}, bf16[3,256,128]{2,1,0:T(8,128)(2,1)S(1)}, u32[]{:S(2)}, u32[]{:S(2)}) collective-permute-start(bf16[3,256,128]{2,1,0:T(8,128)(2,1)S(1)} %get-tuple-element.14), channel_id=1, source_target_pairs={{0,16},{8,24},{16,0},{24,8},{32,48},{40,56},{48,32},{56,40},{64,80... | collective-permute-start | bytes 589832 | tf_op jit(solution)/shard_map/ppermute | solution.py:238
  6.6 9.5 %collective-permute-start.2 = (bf16[3,256,128]{2,1,0:T(8,128)(2,1)S(1)}, bf16[3,256,128]{2,1,0:T(8,128)(2,1)S(1)}, u32[]{:S(2)}, u32[]{:S(2)}) collective-permute-start(bf16[3,256,128]{2,1,0:T(8,128)(2,1)S(1)} %edge.1), channel_id=1, source_target_pairs={{0,224},{8,232},{16,48},{24,56},{32,0},{40,8},{48,80},{56,88},{64,... | collective-permute-start | bytes 589832 | tf_op jit(solution)/shard_map/ppermute | solution.py:251
  12.2 8.9 %collective-permute-start = (bf16[3,256,128]{2,1,0:T(8,128)(2,1)S(1)}, bf16[3,256,128]{2,1,0:T(8,128)(2,1)S(1)}, u32[]{:S(2)}, u32[]{:S(2)}) collective-permute-start(bf16[3,256,128]{2,1,0:T(8,128)(2,1)S(1)} %get-tuple-element.10), channel_id=1, source_target_pairs={{0,24},{8,16},{16,8},{24,0},{32,56},{40,48},{48,40},{56,32},{64,88... | collective-permute-start | bytes 589832 | tf_op jit(solution)/shard_map/ppermute | solution.py:238
  12.9 1.0 %copy-start.1 = (bf16[512,256]{1,0:T(8,128)(2,1)S(1)}, bf16[512,256]{1,0:T(8,128)(2,1)}, u32[]{:S(2)}) copy-start(bf16[512,256]{1,0:T(8,128)(2,1)} %constant.8.clone.fh) | copy-start | bytes 786436
  14.8 6.3 %copy-start.2 = (bf16[512,256]{1,0:T(8,128)(2,1)S(1)}, bf16[512,256]{1,0:T(8,128)(2,1)}, u32[]{:S(2)}) copy-start(bf16[512,256]{1,0:T(8,128)(2,1)} %constant.8.clone.fh) | copy-start | bytes 786436
  14.8 6.3 %copy-start.3 = (bf16[256,512]{1,0:T(8,128)(2,1)S(1)}, bf16[256,512]{1,0:T(8,128)(2,1)}, u32[]{:S(2)}) copy-start(bf16[256,512]{1,0:T(8,128)(2,1)} %constant.11.clone.il) | copy-start | bytes 786436
  14.8 6.3 %copy-start.4 = (bf16[256,512]{1,0:T(8,128)(2,1)S(1)}, bf16[256,512]{1,0:T(8,128)(2,1)}, u32[]{:S(2)}) copy-start(bf16[256,512]{1,0:T(8,128)(2,1)} %constant.10.clone.ih) | copy-start | bytes 786436
  21.1 14.5 %copy-start.5 = (s32[512]{0:T(512)S(1)}, s32[512]{0:T(512)}, u32[]{:S(2)}) copy-start(s32[512]{0:T(512)} %param.8) | copy-start | bytes 6148

commit v7 on v6

--- a/solution.py
+++ b/solution.py
@@ -250,7 +250,14 @@
     hops = [(s, (s - GROUP if s % GROUP < 2 else s + GROUP) % count) for s in range(count)]
     near = lax.ppermute(edge, "tm", hops)
 
-    order = [z * GROUP + x * 2 + c for x in (1, 0) for z in range(count // GROUP)[::-1] for c in (1, 0)]
+    zs = list(range(count // GROUP))[::-1]
+    order = [
+        z * GROUP + x * 2 + c
+        for part in (zs[: len(zs) // 2], zs[len(zs) // 2 :])
+        for x in (1, 0)
+        for z in part
+        for c in (1, 0)
+    ]
     (fh, fl), (ih, il) = tables(order, per)
     early, before = pl.pallas_call(
         early_kernel,
@@ -300,7 +307,7 @@
         name="sums",
     )(valid_frames, mask, parts)
     everyone = lax.all_to_all(
-        sums, "comp", 0, 0, tiled=True, axis_index_groups=[[y * 2 + x for y in (2, 3, 1, 0) for x in (1, 0)]]
+        sums, "comp", 0, 0, tiled=True, axis_index_groups=[[y * 2 + x for y in (2, 1, 3, 0) for x in (1, 0)]]
     )
     correlation, average = pl.pallas_call(
         functools.partial(finish_kernel, order),

time: 43.9 us -> 43.6 us (level)
  no operation moved by 1% of the time
where the time goes in v7:
time: 43.6 us; the launch traced here: 43.3 us
  blocking collectives  20.3 us (47%)
  starting transfers between devices  9.98 us (23%)
  waiting for transfers between devices  5.34 us (12%)
  Pallas kernels  5.31 us (12%)
  between operations  1.39 us (3%)
  local copies, waits for them, and re-layouts  0.98 us (2%)
    all_to_all x1, blocking collectives, body(): lax.all_to_all(lag_sums.reshape(count, per, LANES), 'tm', 0, 0, tiled=Tru...  13 us
    all_to_all x1, blocking collectives, body(): lax.all_to_all(sums, 'comp', 0, 0, tiled=True, axis_index_groups=[[y * 2...  7.31 us
    ppermute x1, starting transfers between devices, body(): near = lax.ppermute(edge, 'tm', hops)  5.62 us
    ppermute x3, starting transfers between devices, swapped(): return lax.ppermute(piece, 'tm', [(s, s ^ k) for s in range(count)])  4.36 us
    ppermute x3, waiting for transfers between devices, swapped(): return lax.ppermute(piece, 'tm', [(s, s ^ k) for s in range(count)])  4.07 us
    pallas_call x1, Pallas kernels, body(): pl.pallas_call(functools.partial(pieces_kernel, order), out_shape=(block,...  1.32 us
    ppermute x1, waiting for transfers between devices, body(): near = lax.ppermute(edge, 'tm', hops)  1.27 us
    pallas_call x1, Pallas kernels, body(): pl.pallas_call(late_kernel, out_shape=f32(LAGS, LANES), in_specs=[smem] +...  1.12 us
  transfers between devices with their start and end apart: 4, of which 2 were waited for; matrix products, arithmetic and copies ran while one was open for 0% of the time, Pallas kernels for 5%

profile of v7, /device:TPU:1, one launch (start us, length us, event | category | flops | bytes accessed | tf_op | source)
XLA Modules:
  0.0 43.3 jit_solution(13851603771608967044)
XLA Ops:
  0.6 0.0 copy-start
  0.6 1.3 %pieces.1 = (bf16[3,256,128]{2,1,0:T(8,128)(2,1)S(1)}, bf16[3,256,128]{2,1,0:T(8,128)(2,1)S(1)}, bf16[3,256,128]{2,1,0:T(8,128)(2,1)S(1)}, bf16[3,256,128]{2,1,0:T(8,128)(2,1)S(1)}) custom-call(bf16[3,256,512]{2,1,0:T(8,128)(2,1)} %bitcast.6), custom_call_target="tpu_custom_call" | custom-call | tf_op jit(solution)/shard_map/pieces/pallas_call | solution.py:227
  2.0 3.3 %collective-permute-start.1 = (bf16[3,256,128]{2,1,0:T(8,128)(2,1)S(1)}, bf16[3,256,128]{2,1,0:T(8,128)(2,1)S(1)}, u32[]{:S(2)}, u32[]{:S(2)}) collective-permute-start(bf16[3,256,128]{2,1,0:T(8,128)(2,1)S(1)} %get-tuple-element.12), channel_id=1, source_target_pairs={{0,8},{8,0},{16,24},{24,16},{32,40},{40,32},{48,56},{56,48},{64,72... | collective-permute-start | bytes 589832 | tf_op jit(solution)/shard_map/ppermute | solution.py:238
  5.3 1.0 %collective-permute-start.3 = (bf16[3,256,128]{2,1,0:T(8,128)(2,1)S(1)}, bf16[3,256,128]{2,1,0:T(8,128)(2,1)S(1)}, u32[]{:S(2)}, u32[]{:S(2)}) collective-permute-start(bf16[3,256,128]{2,1,0:T(8,128)(2,1)S(1)} %get-tuple-element.14), channel_id=1, source_target_pairs={{0,16},{8,24},{16,0},{24,8},{32,48},{40,56},{48,32},{56,40},{64,80... | collective-permute-start | bytes 589832 | tf_op jit(solution)/shard_map/ppermute | solution.py:238
  6.3 0.0 collective-permute-done.1.core
  6.4 0.2 edge.1
  6.6 5.6 %collective-permute-start.2 = (bf16[3,256,128]{2,1,0:T(8,128)(2,1)S(1)}, bf16[3,256,128]{2,1,0:T(8,128)(2,1)S(1)}, u32[]{:S(2)}, u32[]{:S(2)}) collective-permute-start(bf16[3,256,128]{2,1,0:T(8,128)(2,1)S(1)} %edge.1), channel_id=1, source_target_pairs={{0,224},{8,232},{16,48},{24,56},{32,0},{40,8},{48,80},{56,88},{64,... | collective-permute-start | bytes 589832 | tf_op jit(solution)/shard_map/ppermute | solution.py:251
  12.2 0.0 collective-permute-start
  12.9 0.0 copy-start.1
  12.9 0.9 %copy-done.1 = bf16[512,256]{1,0:T(8,128)(2,1)S(1)} copy-done((bf16[512,256]{1,0:T(8,128)(2,1)S(1)}, bf16[512,256]{1,0:T(8,128)(2,1)}, u32[]{:S(2)}) %copy-start.1) | copy-done | bytes 262168
  13.8 1.0 %early_blocks.1 = (f32[2,512,384]{2,1,0:T(8,128)S(1)}, f32[512,128]{1,0:T(8,128)S(1)}) custom-call(s32[1]{0:T(128)S(6)} %copy.9.valid_ref, bf16[3,256,128]{2,1,0:T(8,128)(2,1)S(1)} %get-tuple-element.11.own, bf16[3,256,128]{2,1,0:T(8,128)(2,1)S(1)} %collective-permute-done.1.core, bf16[512,256]{1,0:T(8,128)(2,1)S(1)} %copy-done.1, bf16[512,256]{1,0:T(8,128)(2,1)S(1)} %copy-done), custom_call_target="tpu_custom_call" | custom-call | bytes 8000000 | tf_op jit(solution)/shard_map/early_blocks/pallas_call | solution.py:262
  14.8 0.0 copy-start.2
  14.8 0.0 copy-start.3
  14.8 0.0 copy-start.4
  14.9 0.0 collective-permute-done.3.across
  14.9 1.3 %collective-permute-done.2.near = bf16[3,256,128]{2,1,0:T(8,128)(2,1)S(1)} collective-permute-done((bf16[3,256,128]{2,1,0:T(8,128)(2,1)S(1)}, bf16[3,256,128]{2,1,0:T(8,128)(2,1)S(1)}, u32[]{:S(2)}, u32[]{:S(2)}) %collective-permute-start.2) | collective-permute-done | bytes 196640 | tf_op jit(solution)/shard_map/ppermute | solution.py:251
  16.1 1.0 %middle_block.1 = (f32[2,512,384]{2,1,0:T(8,128)S(1)}, f32[512,128]{1,0:T(8,128)S(1)}) custom-call(s32[1]{0:T(128)S(6)} %copy.9.valid_ref, bf16[3,256,128]{2,1,0:T(8,128)(2,1)S(1)} %collective-permute-done.2.near, bf16[3,256,128]{2,1,0:T(8,128)(2,1)S(1)} %collective-permute-done.3.across, f32[2,512,384]{2,1,0:T(8,128)S(1)} %get-tuple-element.13.early, ...), custom_call_target="tpu_custom_call" | custom-call | tf_op jit(solution)/shard_map/middle_block/pallas_call | solution.py:271
  17.1 4.0 %collective-permute-done.corner = bf16[3,256,128]{2,1,0:T(8,128)(2,1)S(1)} collective-permute-done((bf16[3,256,128]{2,1,0:T(8,128)(2,1)S(1)}, bf16[3,256,128]{2,1,0:T(8,128)(2,1)S(1)}, u32[]{:S(2)}, u32[]{:S(2)}) %collective-permute-start) | collective-permute-done | bytes 196640 | tf_op jit(solution)/shard_map/ppermute | solution.py:238
  21.1 0.0 copy-start.5
  21.1 1.1 %lag_sums.1 = f32[256,128]{1,0:T(8,128)S(1)} custom-call(s32[1]{0:T(128)S(6)} %copy.9.valid_ref, bf16[3,256,128]{2,1,0:T(8,128)(2,1)S(1)} %collective-permute-done.corner, f32[2,512,384]{2,1,0:T(8,128)S(1)} %get-tuple-element.13.early, f32[2,512,384]{2,1,0:T(8,128)S(1)} %get-tuple-element.16.middle, f32[512,128]{1,0:T(8,128)S(1)} %get-tuple-element.17.before, ...), custom_call_target="tpu_custom_call" | custom-call | tf_op jit(solution)/shard_map/lag_sums/pallas_call | solution.py:279
  22.3 13.0 %all_to_all.10.parts = f32[32,8,128]{2,1,0:T(8,128)S(1)} all-to-all(f32[32,8,128]{2,1,0:T(8,128)S(1)} %bitcast.3), channel_id=1, replica_groups={{248,240,216,208,184,176,152,144,232,224,200,192,168,160,136,128,120,11..., dimensions={0} | all-to-all | bytes 262144 | tf_op jit(solution)/shard_map/all_to_all | solution.py:292
  35.3 0.1 sums.1
  35.4 7.3 %all_to_all.11.everyone = f32[8,1,128]{2,1,0:T(1,128)S(1)} all-to-all(f32[8,1,128]{2,1,0:T(1,128)S(1)} %sums.1), channel_id=1, replica_groups={{5,4,3,2,7,6,1,0},{13,12,11,10,15,14,9,8},{21,20,19,18,23,22,17,16},{29..., dimensions={0} | all-to-all | bytes 8192 | tf_op jit(solution)/shard_map/all_to_all | solution.py:309
  42.7 0.6 %finish.1 = (f32[8,512]{1,0:T(8,128)}, f32[8]{0:T(128)}) custom-call(s32[1]{0:T(128)S(6)} %copy.9.valid_ref, s32[1,512]{1,0:T(1,128)S(1)} %bitcast.5, f32[32,8,128]{2,1,0:T(8,128)S(1)} %all_to_all.10.parts, f32[8,1,128]{2,1,0:T(1,128)S(1)} %all_to_all.11.everyone), custom_call_target="tpu_custom_call" | custom-call | tf_op jit(solution)/shard_map/finish/pallas_call | solution.py:312
  (5 shorter events, 0.0 us)
Async XLA Ops:
  0.6 12.2 %copy-start = (bf16[512,256]{1,0:T(8,128)(2,1)S(1)}, bf16[512,256]{1,0:T(8,128)(2,1)}, u32[]{:S(2)}) copy-start(bf16[512,256]{1,0:T(8,128)(2,1)} %constant.9.clone.fl) | copy-start | bytes 786436
  2.0 4.4 %collective-permute-start.1 = (bf16[3,256,128]{2,1,0:T(8,128)(2,1)S(1)}, bf16[3,256,128]{2,1,0:T(8,128)(2,1)S(1)}, u32[]{:S(2)}, u32[]{:S(2)}) collective-permute-start(bf16[3,256,128]{2,1,0:T(8,128)(2,1)S(1)} %get-tuple-element.12), channel_id=1, source_target_pairs={{0,8},{8,0},{16,24},{24,16},{32,40},{40,32},{48,56},{56,48},{64,72... | collective-permute-start | bytes 589832 | tf_op jit(solution)/shard_map/ppermute | solution.py:238
  5.3 9.6 %collective-permute-start.3 = (bf16[3,256,128]{2,1,0:T(8,128)(2,1)S(1)}, bf16[3,256,128]{2,1,0:T(8,128)(2,1)S(1)}, u32[]{:S(2)}, u32[]{:S(2)}) collective-permute-start(bf16[3,256,128]{2,1,0:T(8,128)(2,1)S(1)} %get-tuple-element.14), channel_id=1, source_target_pairs={{0,16},{8,24},{16,0},{24,8},{32,48},{40,56},{48,32},{56,40},{64,80... | collective-permute-start | bytes 589832 | tf_op jit(solution)/shard_map/ppermute | solution.py:238
  6.6 9.5 %collective-permute-start.2 = (bf16[3,256,128]{2,1,0:T(8,128)(2,1)S(1)}, bf16[3,256,128]{2,1,0:T(8,128)(2,1)S(1)}, u32[]{:S(2)}, u32[]{:S(2)}) collective-permute-start(bf16[3,256,128]{2,1,0:T(8,128)(2,1)S(1)} %edge.1), channel_id=1, source_target_pairs={{0,224},{8,232},{16,48},{24,56},{32,0},{40,8},{48,80},{56,88},{64,... | collective-permute-start | bytes 589832 | tf_op jit(solution)/shard_map/ppermute | solution.py:251
  12.2 8.9 %collective-permute-start = (bf16[3,256,128]{2,1,0:T(8,128)(2,1)S(1)}, bf16[3,256,128]{2,1,0:T(8,128)(2,1)S(1)}, u32[]{:S(2)}, u32[]{:S(2)}) collective-permute-start(bf16[3,256,128]{2,1,0:T(8,128)(2,1)S(1)} %get-tuple-element.10), channel_id=1, source_target_pairs={{0,24},{8,16},{16,8},{24,0},{32,56},{40,48},{48,40},{56,32},{64,88... | collective-permute-start | bytes 589832 | tf_op jit(solution)/shard_map/ppermute | solution.py:238
  12.9 1.0 %copy-start.1 = (bf16[512,256]{1,0:T(8,128)(2,1)S(1)}, bf16[512,256]{1,0:T(8,128)(2,1)}, u32[]{:S(2)}) copy-start(bf16[512,256]{1,0:T(8,128)(2,1)} %constant.8.clone.fh) | copy-start | bytes 786436
  14.8 6.3 %copy-start.2 = (bf16[512,256]{1,0:T(8,128)(2,1)S(1)}, bf16[512,256]{1,0:T(8,128)(2,1)}, u32[]{:S(2)}) copy-start(bf16[512,256]{1,0:T(8,128)(2,1)} %constant.8.clone.fh) | copy-start | bytes 786436
  14.8 6.3 %copy-start.3 = (bf16[256,512]{1,0:T(8,128)(2,1)S(1)}, bf16[256,512]{1,0:T(8,128)(2,1)}, u32[]{:S(2)}) copy-start(bf16[256,512]{1,0:T(8,128)(2,1)} %constant.11.clone.il) | copy-start | bytes 786436
  14.8 6.3 %copy-start.4 = (bf16[256,512]{1,0:T(8,128)(2,1)S(1)}, bf16[256,512]{1,0:T(8,128)(2,1)}, u32[]{:S(2)}) copy-start(bf16[256,512]{1,0:T(8,128)(2,1)} %constant.10.clone.ih) | copy-start | bytes 786436
  21.1 14.2 %copy-start.5 = (s32[512]{0:T(512)S(1)}, s32[512]{0:T(512)}, u32[]{:S(2)}) copy-start(s32[512]{0:T(512)} %param.8) | copy-start | bytes 6148

commit v8 on v7

--- a/solution.py
+++ b/solution.py
@@ -56,7 +56,7 @@
     into[slot] = dot(fh[...], clean) + dot(fl[...], clean)
 
 
-def products(power, before, blocks, alone, pairs, rows=32):
+def products(power, before, blocks, alone, pairs, rows=64):
     half = SIZE // 2
     for parity in range(2):
 
@@ -307,7 +307,7 @@
         name="sums",
     )(valid_frames, mask, parts)
     everyone = lax.all_to_all(
-        sums, "comp", 0, 0, tiled=True, axis_index_groups=[[y * 2 + x for y in (2, 1, 3, 0) for x in (1, 0)]]
+        sums, "comp", 0, 0, tiled=True, axis_index_groups=[[y * 2 + x for x in (1, 0) for y in (2, 1, 3, 0)]]
     )
     correlation, average = pl.pallas_call(
         functools.partial(finish_kernel, order),

time: 43.6 us -> 43.5 us (level)
  no operation moved by 1% of the time
where the time goes in v8:
time: 43.5 us; the launch traced here: 43.3 us
  blocking collectives  20.3 us (47%)
  starting transfers between devices  9.98 us (23%)
  waiting for transfers between devices  5.39 us (12%)
  Pallas kernels  5.23 us (12%)
  between operations  1.39 us (3%)
  local copies, waits for them, and re-layouts  0.98 us (2%)
    all_to_all x1, blocking collectives, body(): lax.all_to_all(lag_sums.reshape(count, per, LANES), 'tm', 0, 0, tiled=Tru...  13 us
    all_to_all x1, blocking collectives, body(): lax.all_to_all(sums, 'comp', 0, 0, tiled=True, axis_index_groups=[[y * 2...  7.32 us
    ppermute x1, starting transfers between devices, body(): near = lax.ppermute(edge, 'tm', hops)  5.62 us
    ppermute x3, starting transfers between devices, swapped(): return lax.ppermute(piece, 'tm', [(s, s ^ k) for s in range(count)])  4.36 us
    ppermute x3, waiting for transfers between devices, swapped(): return lax.ppermute(piece, 'tm', [(s, s ^ k) for s in range(count)])  4.1 us
    pallas_call x1, Pallas kernels, body(): pl.pallas_call(functools.partial(pieces_kernel, order), out_shape=(block,...  1.32 us
    ppermute x1, waiting for transfers between devices, body(): near = lax.ppermute(edge, 'tm', hops)  1.3 us
    pallas_call x1, Pallas kernels, body(): pl.pallas_call(late_kernel, out_shape=f32(LAGS, LANES), in_specs=[smem] +...  1.08 us
  transfers between devices with their start and end apart: 4, of which 2 were waited for; matrix products, arithmetic and copies ran while one was open for 0% of the time, Pallas kernels for 5%

profile of v8, /device:TPU:1, one launch (start us, length us, event | category | flops | bytes accessed | tf_op | source)
XLA Modules:
  0.0 43.3 jit_solution(1302694049551020672)
XLA Ops:
  0.6 0.0 copy-start
  0.6 1.3 %pieces.1 = (bf16[3,256,128]{2,1,0:T(8,128)(2,1)S(1)}, bf16[3,256,128]{2,1,0:T(8,128)(2,1)S(1)}, bf16[3,256,128]{2,1,0:T(8,128)(2,1)S(1)}, bf16[3,256,128]{2,1,0:T(8,128)(2,1)S(1)}) custom-call(bf16[3,256,512]{2,1,0:T(8,128)(2,1)} %bitcast.6), custom_call_target="tpu_custom_call" | custom-call | tf_op jit(solution)/shard_map/pieces/pallas_call | solution.py:227
  2.0 3.3 %collective-permute-start.1 = (bf16[3,256,128]{2,1,0:T(8,128)(2,1)S(1)}, bf16[3,256,128]{2,1,0:T(8,128)(2,1)S(1)}, u32[]{:S(2)}, u32[]{:S(2)}) collective-permute-start(bf16[3,256,128]{2,1,0:T(8,128)(2,1)S(1)} %get-tuple-element.12), channel_id=1, source_target_pairs={{0,8},{8,0},{16,24},{24,16},{32,40},{40,32},{48,56},{56,48},{64,72... | collective-permute-start | bytes 589832 | tf_op jit(solution)/shard_map/ppermute | solution.py:238
  5.3 1.0 %collective-permute-start.3 = (bf16[3,256,128]{2,1,0:T(8,128)(2,1)S(1)}, bf16[3,256,128]{2,1,0:T(8,128)(2,1)S(1)}, u32[]{:S(2)}, u32[]{:S(2)}) collective-permute-start(bf16[3,256,128]{2,1,0:T(8,128)(2,1)S(1)} %get-tuple-element.14), channel_id=1, source_target_pairs={{0,16},{8,24},{16,0},{24,8},{32,48},{40,56},{48,32},{56,40},{64,80... | collective-permute-start | bytes 589832 | tf_op jit(solution)/shard_map/ppermute | solution.py:238
  6.3 0.0 collective-permute-done.1.core
  6.4 0.2 edge.1
  6.6 5.6 %collective-permute-start.2 = (bf16[3,256,128]{2,1,0:T(8,128)(2,1)S(1)}, bf16[3,256,128]{2,1,0:T(8,128)(2,1)S(1)}, u32[]{:S(2)}, u32[]{:S(2)}) collective-permute-start(bf16[3,256,128]{2,1,0:T(8,128)(2,1)S(1)} %edge.1), channel_id=1, source_target_pairs={{0,224},{8,232},{16,48},{24,56},{32,0},{40,8},{48,80},{56,88},{64,... | collective-permute-start | bytes 589832 | tf_op jit(solution)/shard_map/ppermute | solution.py:251
  12.2 0.0 collective-permute-start
  12.9 0.0 copy-start.1
  12.9 0.9 %copy-done.1 = bf16[512,256]{1,0:T(8,128)(2,1)S(1)} copy-done((bf16[512,256]{1,0:T(8,128)(2,1)S(1)}, bf16[512,256]{1,0:T(8,128)(2,1)}, u32[]{:S(2)}) %copy-start.1) | copy-done | bytes 262168
  13.8 0.9 %early_blocks.1 = (f32[2,512,384]{2,1,0:T(8,128)S(1)}, f32[512,128]{1,0:T(8,128)S(1)}) custom-call(s32[1]{0:T(128)S(6)} %copy.9.valid_ref, bf16[3,256,128]{2,1,0:T(8,128)(2,1)S(1)} %get-tuple-element.11.own, bf16[3,256,128]{2,1,0:T(8,128)(2,1)S(1)} %collective-permute-done.1.core, bf16[512,256]{1,0:T(8,128)(2,1)S(1)} %copy-done.1, bf16[512,256]{1,0:T(8,128)(2,1)S(1)} %copy-done), custom_call_target="tpu_custom_call" | custom-call | bytes 8000000 | tf_op jit(solution)/shard_map/early_blocks/pallas_call | solution.py:262
  14.8 0.0 copy-start.2
  14.8 0.0 copy-start.3
  14.8 0.0 copy-start.4
  14.8 0.0 collective-permute-done.3.across
  14.8 1.3 %collective-permute-done.2.near = bf16[3,256,128]{2,1,0:T(8,128)(2,1)S(1)} collective-permute-done((bf16[3,256,128]{2,1,0:T(8,128)(2,1)S(1)}, bf16[3,256,128]{2,1,0:T(8,128)(2,1)S(1)}, u32[]{:S(2)}, u32[]{:S(2)}) %collective-permute-start.2) | collective-permute-done | bytes 196640 | tf_op jit(solution)/shard_map/ppermute | solution.py:251
  16.1 0.9 %middle_block.1 = (f32[2,512,384]{2,1,0:T(8,128)S(1)}, f32[512,128]{1,0:T(8,128)S(1)}) custom-call(s32[1]{0:T(128)S(6)} %copy.9.valid_ref, bf16[3,256,128]{2,1,0:T(8,128)(2,1)S(1)} %collective-permute-done.2.near, bf16[3,256,128]{2,1,0:T(8,128)(2,1)S(1)} %collective-permute-done.3.across, f32[2,512,384]{2,1,0:T(8,128)S(1)} %get-tuple-element.13.early, ...), custom_call_target="tpu_custom_call" | custom-call | tf_op jit(solution)/shard_map/middle_block/pallas_call | solution.py:271
  17.1 4.0 %collective-permute-done.corner = bf16[3,256,128]{2,1,0:T(8,128)(2,1)S(1)} collective-permute-done((bf16[3,256,128]{2,1,0:T(8,128)(2,1)S(1)}, bf16[3,256,128]{2,1,0:T(8,128)(2,1)S(1)}, u32[]{:S(2)}, u32[]{:S(2)}) %collective-permute-start) | collective-permute-done | bytes 196640 | tf_op jit(solution)/shard_map/ppermute | solution.py:238
  21.1 0.0 copy-start.5
  21.1 1.1 %lag_sums.1 = f32[256,128]{1,0:T(8,128)S(1)} custom-call(s32[1]{0:T(128)S(6)} %copy.9.valid_ref, bf16[3,256,128]{2,1,0:T(8,128)(2,1)S(1)} %collective-permute-done.corner, f32[2,512,384]{2,1,0:T(8,128)S(1)} %get-tuple-element.13.early, f32[2,512,384]{2,1,0:T(8,128)S(1)} %get-tuple-element.16.middle, f32[512,128]{1,0:T(8,128)S(1)} %get-tuple-element.17.before, ...), custom_call_target="tpu_custom_call" | custom-call | tf_op jit(solution)/shard_map/lag_sums/pallas_call | solution.py:279
  22.2 13.0 %all_to_all.10.parts = f32[32,8,128]{2,1,0:T(8,128)S(1)} all-to-all(f32[32,8,128]{2,1,0:T(8,128)S(1)} %bitcast.3), channel_id=1, replica_groups={{248,240,216,208,184,176,152,144,232,224,200,192,168,160,136,128,120,11..., dimensions={0} | all-to-all | bytes 262144 | tf_op jit(solution)/shard_map/all_to_all | solution.py:292
  35.3 0.1 sums.1
  35.4 7.3 %all_to_all.11.everyone = f32[8,1,128]{2,1,0:T(1,128)S(1)} all-to-all(f32[8,1,128]{2,1,0:T(1,128)S(1)} %sums.1), channel_id=1, replica_groups={{5,3,7,1,4,2,6,0},{13,11,15,9,12,10,14,8},{21,19,23,17,20,18,22,16},{29..., dimensions={0} | all-to-all | bytes 8192 | tf_op jit(solution)/shard_map/all_to_all | solution.py:309
  42.7 0.6 %finish.1 = (f32[8,512]{1,0:T(8,128)}, f32[8]{0:T(128)}) custom-call(s32[1]{0:T(128)S(6)} %copy.9.valid_ref, s32[1,512]{1,0:T(1,128)S(1)} %bitcast.5, f32[32,8,128]{2,1,0:T(8,128)S(1)} %all_to_all.10.parts, f32[8,1,128]{2,1,0:T(1,128)S(1)} %all_to_all.11.everyone), custom_call_target="tpu_custom_call" | custom-call | tf_op jit(solution)/shard_map/finish/pallas_call | solution.py:312
  (5 shorter events, 0.0 us)
Async XLA Ops:
  0.6 12.2 %copy-start = (bf16[512,256]{1,0:T(8,128)(2,1)S(1)}, bf16[512,256]{1,0:T(8,128)(2,1)}, u32[]{:S(2)}) copy-start(bf16[512,256]{1,0:T(8,128)(2,1)} %constant.9.clone.fl) | copy-start | bytes 786436
  2.0 4.4 %collective-permute-start.1 = (bf16[3,256,128]{2,1,0:T(8,128)(2,1)S(1)}, bf16[3,256,128]{2,1,0:T(8,128)(2,1)S(1)}, u32[]{:S(2)}, u32[]{:S(2)}) collective-permute-start(bf16[3,256,128]{2,1,0:T(8,128)(2,1)S(1)} %get-tuple-element.12), channel_id=1, source_target_pairs={{0,8},{8,0},{16,24},{24,16},{32,40},{40,32},{48,56},{56,48},{64,72... | collective-permute-start | bytes 589832 | tf_op jit(solution)/shard_map/ppermute | solution.py:238
  5.3 9.5 %collective-permute-start.3 = (bf16[3,256,128]{2,1,0:T(8,128)(2,1)S(1)}, bf16[3,256,128]{2,1,0:T(8,128)(2,1)S(1)}, u32[]{:S(2)}, u32[]{:S(2)}) collective-permute-start(bf16[3,256,128]{2,1,0:T(8,128)(2,1)S(1)} %get-tuple-element.14), channel_id=1, source_target_pairs={{0,16},{8,24},{16,0},{24,8},{32,48},{40,56},{48,32},{56,40},{64,80... | collective-permute-start | bytes 589832 | tf_op jit(solution)/shard_map/ppermute | solution.py:238
  6.6 9.5 %collective-permute-start.2 = (bf16[3,256,128]{2,1,0:T(8,128)(2,1)S(1)}, bf16[3,256,128]{2,1,0:T(8,128)(2,1)S(1)}, u32[]{:S(2)}, u32[]{:S(2)}) collective-permute-start(bf16[3,256,128]{2,1,0:T(8,128)(2,1)S(1)} %edge.1), channel_id=1, source_target_pairs={{0,224},{8,232},{16,48},{24,56},{32,0},{40,8},{48,80},{56,88},{64,... | collective-permute-start | bytes 589832 | tf_op jit(solution)/shard_map/ppermute | solution.py:251
  12.2 8.9 %collective-permute-start = (bf16[3,256,128]{2,1,0:T(8,128)(2,1)S(1)}, bf16[3,256,128]{2,1,0:T(8,128)(2,1)S(1)}, u32[]{:S(2)}, u32[]{:S(2)}) collective-permute-start(bf16[3,256,128]{2,1,0:T(8,128)(2,1)S(1)} %get-tuple-element.10), channel_id=1, source_target_pairs={{0,24},{8,16},{16,8},{24,0},{32,56},{40,48},{48,40},{56,32},{64,88... | collective-permute-start | bytes 589832 | tf_op jit(solution)/shard_map/ppermute | solution.py:238
  12.9 1.0 %copy-start.1 = (bf16[512,256]{1,0:T(8,128)(2,1)S(1)}, bf16[512,256]{1,0:T(8,128)(2,1)}, u32[]{:S(2)}) copy-start(bf16[512,256]{1,0:T(8,128)(2,1)} %constant.8.clone.fh) | copy-start | bytes 786436
  14.8 6.3 %copy-start.2 = (bf16[512,256]{1,0:T(8,128)(2,1)S(1)}, bf16[512,256]{1,0:T(8,128)(2,1)}, u32[]{:S(2)}) copy-start(bf16[512,256]{1,0:T(8,128)(2,1)} %constant.8.clone.fh) | copy-start | bytes 786436
  14.8 6.3 %copy-start.3 = (bf16[256,512]{1,0:T(8,128)(2,1)S(1)}, bf16[256,512]{1,0:T(8,128)(2,1)}, u32[]{:S(2)}) copy-start(bf16[256,512]{1,0:T(8,128)(2,1)} %constant.11.clone.il) | copy-start | bytes 786436
  14.8 6.3 %copy-start.4 = (bf16[256,512]{1,0:T(8,128)(2,1)S(1)}, bf16[256,512]{1,0:T(8,128)(2,1)}, u32[]{:S(2)}) copy-start(bf16[256,512]{1,0:T(8,128)(2,1)} %constant.10.clone.ih) | copy-start | bytes 786436
  21.1 14.1 %copy-start.5 = (s32[512]{0:T(512)S(1)}, s32[512]{0:T(512)}, u32[]{:S(2)}) copy-start(s32[512]{0:T(512)} %param.8) | copy-start | bytes 6148
